TPU v7x, 256 devices: a whole 4x4x8 slice. The times are simulated.
256 devices in a mesh: dp: 4 (over x), shard: 64 (over y, z, core).
Axes of the slice: x: 4, y: 4, z: 8, core: 2. Of those that a mesh axis runs over, the one named last changes fastest.
Arguments:
- grads: bfloat16 [4, 256, 512, 512], P('dp', None, 'shard'), may hold values from -5 to 5
- owner: int32 [256, 1], replicated, may hold values from 0 to 63; in each aligned block of 64 rows (0 to 63, 64 to 127, ...) at most 2 rows name the same one
- left_factor: float32 [4, 64, 2, 512, 512], P('dp', 'shard'), may hold values from -6 to 6
- right_factor: float32 [4, 64, 2, 512, 512], P('dp', 'shard'), may hold values from -6 to 6
- left_root: bfloat16 [4, 64, 2, 512, 512], P('dp', 'shard'), may hold values from -0.25 to 0.25
- right_root: bfloat16 [4, 64, 2, 512, 512], P('dp', 'shard'), may hold values from -0.25 to 0.25
Outputs:
- new_left: float32 [4, 64, 2, 512, 512], P('dp', 'shard')
- new_right: float32 [4, 64, 2, 512, 512], P('dp', 'shard')
- update: bfloat16 [256, 512, 512], P('dp', 'shard')
Inputs may be any that keep to these rules, and one draw needn't show every extreme that they name: In each aligned block of 64 entries no owner appears more than 2 times.
All inputs are finite; a program needn't handle non-finite values.
Results may differ from a plain program's by a relative error of at most 0.019.
Values may be sent and summed in bfloat16 or wider, within the bound.
No kernel may reach another device: no remote copies, remote signals or barrier semaphores. Data moves between devices by JAX's collectives and lax.ppermute only.
A program may use at most 64 MiB of HBM per device.

v0:
```python
import jax
import jax.numpy as jnp
from jax import lax
from jax.sharding import PartitionSpec as P

BETA = 0.95
EPS = 1e-06


def shards(grads, owner, left_factor, right_factor, left_root, right_root):
    replicas = lax.axis_size("dp")
    owners = lax.axis_size("shard")
    rows = grads.shape[2]
    width = grads.shape[3]
    group = grads.shape[1] // replicas
    slots_each = left_factor.shape[2]
    total = lax.psum_scatter(
        grads[0].astype(jnp.float32).astype(jnp.bfloat16), "dp", scatter_dimension=0, tiled=True
    ).astype(jnp.float32)
    mean_grad = (total / replicas).astype(jnp.bfloat16)
    table = lax.dynamic_slice_in_dim(owner[:, 0], lax.axis_index("dp") * group, group)
    index = jnp.arange(group, dtype=jnp.int32)
    same = (table[:, None] == table[None, :]) & (index[None, :] < index[:, None])
    slots = jnp.sum(same.astype(jnp.int32), axis=1)
    target = table * slots_each + slots
    selector = (
        jnp.arange(owners * slots_each, dtype=jnp.int32)[:, None] == target[None, :]
    ).astype(jnp.bfloat16)
    outgoing = jnp.dot(
        selector, mean_grad.reshape(group, rows * width), preferred_element_type=jnp.float32
    )
    outgoing = outgoing.astype(jnp.bfloat16).reshape(owners, slots_each, rows, width)
    arrived = lax.all_to_all(outgoing, "shard", split_axis=0, concat_axis=2, tiled=True)
    blocks = arrived[0]
    count = jnp.sum((table == lax.axis_index("shard")).astype(jnp.int32))
    filled = (jnp.arange(slots_each, dtype=jnp.int32) < count)[:, None, None]
    left = left_factor[0, 0]
    right = right_factor[0, 0]
    gram_left = jnp.einsum("cij,ckj->cik", blocks, blocks, preferred_element_type=jnp.float32)
    gram_right = jnp.einsum("cji,cjk->cik", blocks, blocks, preferred_element_type=jnp.float32)
    new_left = jnp.where(filled, BETA * left + (1.0 - BETA) * gram_left, left)
    new_right = jnp.where(filled, BETA * right + (1.0 - BETA) * gram_right, right)
    half = jnp.einsum(
        "cij,cjk->cik", left_root[0, 0], blocks, preferred_element_type=jnp.float32
    ).astype(jnp.bfloat16)
    pre = jnp.einsum("cij,cjk->cik", half, right_root[0, 0], preferred_element_type=jnp.float32)
    grad_power = jnp.mean(jnp.square(blocks.astype(jnp.float32)), axis=(1, 2), keepdims=True)
    pre_power = jnp.mean(pre * pre, axis=(1, 2), keepdims=True)
    finished = (pre * (jnp.sqrt(grad_power + EPS) / jnp.sqrt(pre_power + EPS))).astype(jnp.bfloat16)
    returned = lax.all_to_all(
        finished.reshape(slots_each, owners, rows, width),
        "shard",
        split_axis=1,
        concat_axis=0,
        tiled=True,
    )
    mine = jnp.dot(
        selector.T,
        returned.reshape(owners * slots_each, rows * width),
        preferred_element_type=jnp.float32,
    )
    update = mine.astype(jnp.bfloat16).reshape(group, rows, width)
    return (new_left[None, None], new_right[None, None], update)


def solution(mesh):
    placed = (
        P("dp", None, "shard", None),
        P(),
        P("dp", "shard", None, None, None),
        P("dp", "shard", None, None, None),
        P("dp", "shard", None, None, None),
        P("dp", "shard", None, None, None),
    )
    return jax.shard_map(
        shards,
        mesh=mesh,
        in_specs=placed,
        out_specs=(
            P("dp", "shard", None, None, None),
            P("dp", "shard", None, None, None),
            P("dp", "shard", None),
        ),
        check_vma=False,
    )
```

profile of v0, /device:TPU:1, one launch (start us, length us, event | category | flops | bytes accessed | tf_op | source)
XLA Modules:
  0.0 138.6 jit_solution(9732305666292707896)
XLA Ops:
  7.2 0.0 copy-start
  7.2 0.0 reduce-scatter.2.cloned.1.call-start
  7.2 0.7 reduce-scatter.2.cloned.1.call-update
  7.9 0.0 copy-done.1
  7.9 0.7 fusion.20
  8.6 0.2 convert_reduce_fusion
  8.8 37.8 %reduce-scatter.2.cloned.1.call-done = bf16[64,8,512]{2,1,0:T(8,128)(2,1)} async-done(((bf16[256,8,512]{2,1,0:T(8,128)(2,1)}), bf16[64,8,512]{2,1,0:T(8,128)(2,1)}) %reduce-scatter.2.cloned.1.call-update) | async-done | bytes 524304 | tf_op jit(solution)/shard_map/reduce_scatter | solution.py:17
  46.7 1.1 multiply_convert_fusion.1
  47.8 0.2 copy.22
  48.0 0.4 convolution_convert_fusion
  48.4 0.4 copy.23
  48.8 39.0 %all_to_all.30 = bf16[64,2,8,512]{3,2,1,0:T(8,128)(2,1)S(1)} all-to-all(bf16[64,2,8,512]{3,2,1,0:T(8,128)(2,1)S(1)} %bitcast.82), channel_id=1, replica_groups=mesh['dp'=4,'shard'=64] {'shard'}, dimensions={0} | all-to-all | bytes 2097152 | tf_op jit(solution)/shard_map/all_to_all | solution.py:33
  87.8 0.4 multiply_reduce_fusion.1
  88.2 4.0 %multiply_reduce_fusion = (f32[2]{0:T(128)S(1)}, f32[2,512,512]{2,1,0:T(8,128)}) fusion(bf16[1,1,2,512,512]{4,3,2,1,0:T(8,128)(2,1)S(1)} %copy-done, bf16[1,1,2,512,512]{4,3,2,1,0:T(8,128)(2,1)} %param.10, bf16[64,2,8,512]{3,2,1,0:T(8,128)(2,1)S(1)} %all_to_all.30), kind=kOutput, calls=%fused_computation.11 | convolution fusion | flops 1075314688 | bytes 5242888 | tf_op jit(solution)/shard_map/cij,cjk->cik/dot_general | solution.py:46
  92.2 1.9 %fusion.5 = bf16[2,64,8,512]{3,2,1,0:T(8,128)(2,1)S(1)} fusion(f32[2,512,512]{2,1,0:T(8,128)} %get-tuple-element.6, f32[2]{0:T(128)S(1)} %rsqrt_multiply_fusion), kind=kLoop, calls=%fused_computation.15 | loop fusion | flops 1048576 | bytes 3145736 | tf_op jit(solution)/shard_map/reshape | solution.py:51
  94.1 1.1 copy.18
  95.2 6.2 %all-to-all-start.1 = ((bf16[2,64,8,512]{3,2,0,1:T(8,128)(2,1)}), bf16[2,64,8,512]{3,2,0,1:T(8,128)(2,1)S(1)}, u32[]{:S(2)}, u32[]{:S(2)}) async-start(bf16[2,64,8,512]{3,2,0,1:T(8,128)(2,1)} %copy.18), calls=%async_computation.2 | async-start | bytes 2097152 | tf_op jit(solution)/shard_map/all_to_all | solution.py:50
  101.4 0.7 iota_compare_fusion.4
  102.1 3.9 %fusion.1 = f32[1,1,2,512,512]{4,3,2,1,0:T(8,128)} fusion(f32[1,1,2,512,512]{4,3,2,1,0:T(8,128)} %param.9, pred[2]{0:T(512)(128)(4,1)S(1)} %iota_compare_fusion.4, bf16[64,2,8,512]{3,2,1,0:T(8,128)(2,1)S(1)} %all_to_all.30), kind=kOutput, calls=%fused_computation.5 | convolution fusion | flops 538968064 | bytes 5242882 | tf_op jit(solution)/shard_map/cji,cjk->cik/dot_general | solution.py:40
  106.0 2.3 %fusion.3 = f32[1,1,2,512,512]{4,3,2,1,0:T(8,128)} fusion(f32[1,1,2,512,512]{4,3,2,1,0:T(8,128)S(1)} %copy-done.2, pred[2]{0:T(512)(128)(4,1)S(1)} %iota_compare_fusion.4, bf16[64,2,8,512]{3,2,1,0:T(8,128)(2,1)S(1)} %all_to_all.30), kind=kOutput, calls=%fused_computation.9 | convolution fusion | flops 538968064 | bytes 5242882 | tf_op jit(solution)/shard_map/cij,ckj->cik/dot_general | solution.py:39
  108.3 21.7 %all-to-all-done.1 = bf16[2,64,8,512]{3,2,0,1:T(8,128)(2,1)S(1)} async-done(((bf16[2,64,8,512]{3,2,0,1:T(8,128)(2,1)}), bf16[2,64,8,512]{3,2,0,1:T(8,128)(2,1)S(1)}, u32[]{:S(2)}, u32[]{:S(2)}) %all-to-all-start.1) | async-done | bytes 1048608 | tf_op jit(solution)/shard_map/all_to_all | solution.py:50
  130.0 0.4 copy.24
  130.4 0.3 convolution_convert_fusion.1
  130.7 1.0 copy.25
  (6 shorter events, 0.0 us)
Async XLA Ops:
  7.2 81.0 %copy-start = (bf16[1,1,2,512,512]{4,3,2,1,0:T(8,128)(2,1)S(1)}, bf16[1,1,2,512,512]{4,3,2,1,0:T(8,128)(2,1)}, u32[]{:S(2)}) copy-start(bf16[1,1,2,512,512]{4,3,2,1,0:T(8,128)(2,1)} %param.11) | copy-start | bytes 3145732
  7.2 0.8 copy-start.1
  7.2 39.5 %reduce-scatter.2.cloned.1.call-start = ((), (), s32[]{:S(2)}) async-start(), calls=%async_computation.3 | async-start | bytes 2621440 | tf_op jit(solution)/shard_map/reduce_scatter | solution.py:17
  95.2 34.8 %all-to-all-start.1 = ((bf16[2,64,8,512]{3,2,0,1:T(8,128)(2,1)}), bf16[2,64,8,512]{3,2,0,1:T(8,128)(2,1)S(1)}, u32[]{:S(2)}, u32[]{:S(2)}) async-start(bf16[2,64,8,512]{3,2,0,1:T(8,128)(2,1)} %copy.18), calls=%async_computation.2 | async-start | bytes 2097152 | tf_op jit(solution)/shard_map/all_to_all | solution.py:50
  102.1 3.9 %copy-start.2 = (f32[1,1,2,512,512]{4,3,2,1,0:T(8,128)S(1)}, f32[1,1,2,512,512]{4,3,2,1,0:T(8,128)}, u32[]{:S(2)}) copy-start(f32[1,1,2,512,512]{4,3,2,1,0:T(8,128)} %param.8) | copy-start | bytes 6291460
Sparse Core Ops, SparseCore 0:
  10.6 36.0 reduce-scatter.1
where the time goes:
time: 139 us
  waiting for transfers between devices  60.2 us (43%)
  blocking collectives  39 us (28%)
  between operations  14.1 us (10%)
  matrix products  11 us (8%)
  starting transfers between devices  6.23 us (4%)
  other arithmetic  4.97 us (4%)
  local copies, waits for them, and re-layouts  3.08 us (2%)
    all_to_all x1, blocking collectives, shards(): lax.all_to_all(outgoing, 'shard', split_axis=0, concat_axis=2, tiled=True)  39 us
    reduce_scatter x1, waiting for transfers between devices, shards(): lax.psum_scatter(grads[0].astype(jnp.float32).astype(jnp.bfloat16), 'dp',...  37.8 us
    all_to_all x1, waiting for transfers between devices, shards(): lax.all_to_all(finished.reshape(slots_each, owners, rows, width), 'shard'...  21.7 us
    all_to_all x1, starting transfers between devices, shards(): lax.all_to_all(finished.reshape(slots_each, owners, rows, width), 'shard'...  6.19 us
    dot_general x1, matrix products, shards(): jnp.einsum('cij,cjk->cik', half, right_root[0, 0], preferred_element_type...  3.99 us
    dot_general x1, matrix products, shards(): jnp.einsum('cji,cjk->cik', blocks, blocks, preferred_element_type=jnp.flo...  3.92 us
  transfers between devices with their start and end apart: 2, of which 2 were waited for; matrix products, arithmetic and copies ran while one was open for 6% of the time, Pallas kernels for 0%

commit v1 on v0

v1 whole, which is shorter than its diff:
```python
import jax
import jax.numpy as jnp
from jax import lax
from jax.experimental import pallas as pl
from jax.experimental.pallas import tpu as pltpu
from jax.sharding import PartitionSpec as P

BETA = 0.95
EPS = 1e-06
VMEM_LIMIT = 48 * 1024 * 1024


def mean_and_route(target_ref, parts_ref, out_ref):
    replicas, group = parts_ref.shape[:2]
    out_ref[...] = jnp.zeros_like(out_ref)

    def one(b, _):
        total = parts_ref[0, b].astype(jnp.float32)
        for r in range(1, replicas):
            total = total + parts_ref[r, b].astype(jnp.float32)
        out_ref[target_ref[b]] = (total / replicas).astype(jnp.bfloat16)
        return 0

    lax.fori_loop(0, group, one, 0, unroll=8)


def precondition(arrived_ref, lroot_ref, rroot_ref, out_ref, block):
    senders, slots, rows, width = arrived_ref.shape
    for c in range(slots):
        power = jnp.zeros((rows, width), jnp.float32)
        for s in range(0, senders, 2):
            first = arrived_ref[s, c].astype(jnp.float32)
            second = arrived_ref[s + 1, c].astype(jnp.float32)
            power = power + (first * first + second * second)
            block[pl.ds(s * rows, 2 * rows), :] = jnp.concatenate([first, second], axis=0).astype(jnp.bfloat16)
        half = jnp.dot(lroot_ref[c], block[...], preferred_element_type=jnp.float32).astype(jnp.bfloat16)
        pre = jnp.dot(half, rroot_ref[c], preferred_element_type=jnp.float32)
        entries = senders * rows * width
        grad_power = jnp.sum(power) / entries
        pre_power = jnp.sum(pre * pre) / entries
        ratio = jnp.sqrt(jnp.full((1, 1), grad_power + EPS)) / jnp.sqrt(jnp.full((1, 1), pre_power + EPS))
        finished = pre * ratio
        for s in range(senders):
            out_ref[s, c] = finished[s * rows : (s + 1) * rows].astype(jnp.bfloat16)


def pick(target_ref, returned_ref, out_ref):
    def one(b, _):
        out_ref[b] = returned_ref[target_ref[b]]
        return 0

    lax.fori_loop(0, out_ref.shape[0], one, 0, unroll=8)


def in_vmem():
    return pl.BlockSpec(memory_space=pltpu.VMEM)


def in_smem():
    return pl.BlockSpec(memory_space=pltpu.SMEM)


def params():
    return pltpu.CompilerParams(vmem_limit_bytes=VMEM_LIMIT)


def shards(grads, owner, left_factor, right_factor, left_root, right_root):
    replicas = lax.axis_size("dp")
    owners = lax.axis_size("shard")
    rows = grads.shape[2]
    width = grads.shape[3]
    group = grads.shape[1] // replicas
    slots_each = left_factor.shape[2]
    parts = lax.all_to_all(
        grads[0].reshape(replicas, group, rows, width), "dp", split_axis=0, concat_axis=0, tiled=True
    )
    table = lax.dynamic_slice_in_dim(owner[:, 0], lax.axis_index("dp") * group, group)
    index = jnp.arange(group, dtype=jnp.int32)
    same = (table[:, None] == table[None, :]) & (index[None, :] < index[:, None])
    slots = jnp.sum(same.astype(jnp.int32), axis=1)
    target = table * slots_each + slots
    outgoing = pl.pallas_call(
        mean_and_route,
        out_shape=jax.ShapeDtypeStruct((owners * slots_each, rows, width), jnp.bfloat16),
        in_specs=[in_smem(), in_vmem()],
        out_specs=in_vmem(),
        compiler_params=params(),
    )(target, parts)
    arrived = lax.all_to_all(
        outgoing.reshape(owners, slots_each, rows, width), "shard", split_axis=0, concat_axis=0, tiled=True
    )
    finished = pl.pallas_call(
        precondition,
        out_shape=jax.ShapeDtypeStruct((owners, slots_each, rows, width), jnp.bfloat16),
        in_specs=[in_vmem()] * 3,
        out_specs=in_vmem(),
        scratch_shapes=[pltpu.VMEM((owners * rows, width), jnp.bfloat16)],
        compiler_params=params(),
    )(arrived, left_root[0, 0], right_root[0, 0])
    returned = lax.all_to_all(finished, "shard", split_axis=0, concat_axis=0, tiled=True)
    blocks = arrived.transpose(1, 0, 2, 3).reshape(slots_each, owners * rows, width)
    count = jnp.sum((table == lax.axis_index("shard")).astype(jnp.int32))
    filled = (jnp.arange(slots_each, dtype=jnp.int32) < count)[:, None, None]
    left = left_factor[0, 0]
    right = right_factor[0, 0]
    gram_left = jnp.einsum("cij,ckj->cik", blocks, blocks, preferred_element_type=jnp.float32)
    gram_right = jnp.einsum("cji,cjk->cik", blocks, blocks, preferred_element_type=jnp.float32)
    new_left = jnp.where(filled, BETA * left + (1.0 - BETA) * gram_left, left)
    new_right = jnp.where(filled, BETA * right + (1.0 - BETA) * gram_right, right)
    update = pl.pallas_call(
        pick,
        out_shape=jax.ShapeDtypeStruct((group, rows, width), jnp.bfloat16),
        in_specs=[in_smem(), in_vmem()],
        out_specs=in_vmem(),
        compiler_params=params(),
    )(target, returned.reshape(owners * slots_each, rows, width))
    return (new_left[None, None], new_right[None, None], update)


def solution(mesh):
    placed = (
        P("dp", None, "shard", None),
        P(),
        P("dp", "shard", None, None, None),
        P("dp", "shard", None, None, None),
        P("dp", "shard", None, None, None),
        P("dp", "shard", None, None, None),
    )
    return jax.shard_map(
        shards,
        mesh=mesh,
        in_specs=placed,
        out_specs=(
            P("dp", "shard", None, None, None),
            P("dp", "shard", None, None, None),
            P("dp", "shard", None),
        ),
        check_vma=False,
    )
```

time: 139 us -> 113 us (0.81)
  waiting for transfers between devices: 60.2 us -> 45.1 us
  between operations: 14.1 us -> 0.69 us
  Pallas kernels: 0 us -> 5.16 us
  matrix products: 11 us -> 6.21 us
  starting transfers between devices: 6.23 us -> 11 us
  blocking collectives: 39 us -> 42.9 us
  other arithmetic: 4.97 us -> 1.53 us
  local copies, waits for them, and re-layouts: 3.08 us -> 0.02 us
    reduce_scatter x1 -> x0, waiting for transfers between devices: 37.8 us -> none  [shards(): lax.psum_scatter(grads[0].astype(jnp.float32).astype(jnp.bfloat16), 'dp',...]
    all_to_all x1 -> x2, waiting for transfers between devices: 21.7 us -> 45.1 us  [the longest x1 23.5 us: shards(): lax.all_to_all(grads[0].reshape(replicas, group, rows, width), 'dp', spli...]
    pallas_call x0 -> x3, Pallas kernels: none -> 5.16 us  [the longest x1 2.77 us: shards(): pl.pallas_call(precondition, out_shape=jax.ShapeDtypeStruct((owners, slot...]
    all_to_all x1 -> x2, starting transfers between devices: 6.19 us -> 11 us  [the longest x1 6.18 us: shards(): lax.all_to_all(finished, 'shard', split_axis=0, concat_axis=0, tiled=True)]
    dot_general x3 -> x0, matrix products: 4.76 us -> none  [the longest x1 3.99 us: shards(): jnp.einsum('cij,cjk->cik', half, right_root[0, 0], preferred_element_type...]
    all_to_all x1, blocking collectives: 39 us -> 42.9 us  [shards(): lax.all_to_all(outgoing.reshape(owners, slots_each, rows, width), 'shard'...]
    unnamed x10 -> x8, local copies, waits for them, and re-layouts: 1.97 us -> 0.02 us
    reshape x1 -> x0, other arithmetic: 1.91 us -> none  [shards(): finished.reshape(slots_each, owners, rows, width)]
  transfers between devices with their start and end apart: 2 -> 2, of which waited for: 2 -> 2; matrix products, arithmetic and copies ran while one was open for 6% -> 7% of each run, Pallas kernels for 0% -> 0%
where the time goes in v1:
time: 113 us
  waiting for transfers between devices  45.1 us (40%)
  blocking collectives  42.9 us (38%)
  starting transfers between devices  11 us (10%)
  matrix products  6.21 us (5%)
  Pallas kernels  5.16 us (5%)
  other arithmetic  1.53 us (1%)
    all_to_all x1, blocking collectives, shards(): lax.all_to_all(outgoing.reshape(owners, slots_each, rows, width), 'shard'...  42.9 us
    all_to_all x1, waiting for transfers between devices, shards(): lax.all_to_all(grads[0].reshape(replicas, group, rows, width), 'dp', spli...  23.5 us
    all_to_all x1, waiting for transfers between devices, shards(): lax.all_to_all(finished, 'shard', split_axis=0, concat_axis=0, tiled=True)  21.7 us
    all_to_all x1, starting transfers between devices, shards(): lax.all_to_all(finished, 'shard', split_axis=0, concat_axis=0, tiled=True)  6.18 us
    all_to_all x1, starting transfers between devices, shards(): lax.all_to_all(grads[0].reshape(replicas, group, rows, width), 'dp', spli...  4.85 us
    dot_general x1, matrix products, shards(): jnp.einsum('cji,cjk->cik', blocks, blocks, preferred_element_type=jnp.flo...  3.94 us
    pallas_call x1, Pallas kernels, shards(): pl.pallas_call(precondition, out_shape=jax.ShapeDtypeStruct((owners, slot...  2.77 us
    dot_general x1, matrix products, shards(): jnp.einsum('cij,ckj->cik', blocks, blocks, preferred_element_type=jnp.flo...  2.28 us
  transfers between devices with their start and end apart: 2, of which 2 were waited for; matrix products, arithmetic and copies ran while one was open for 7% of the time, Pallas kernels for 0%

profile of v1, /device:TPU:1, one launch (start us, length us, event | category | flops | bytes accessed | tf_op | source)
XLA Modules:
  0.0 112.7 jit_solution(4784241388802705503)
XLA Ops:
  0.6 0.0 copy-start.2
  0.6 4.9 %all-to-all-start = ((bf16[4,64,8,512]{3,2,1,0:T(8,128)(2,1)}), bf16[4,64,8,512]{3,2,1,0:T(8,128)(2,1)S(1)}, u32[]{:S(2)}, u32[]{:S(2)}) async-start(bf16[4,64,8,512]{3,2,1,0:T(8,128)(2,1)} %bitcast.46), calls=%async_computation | async-start | bytes 4194304 | tf_op jit(solution)/shard_map/all_to_all | solution.py:74
  5.5 0.0 copy-done.2
  5.5 0.7 fusion.9
  6.2 0.2 convert_reduce_fusion
  6.4 0.0 copy-start
  6.4 23.5 %all-to-all-done.parts_ref = bf16[4,64,8,512]{3,2,1,0:T(8,128)(2,1)S(1)} async-done(((bf16[4,64,8,512]{3,2,1,0:T(8,128)(2,1)}), bf16[4,64,8,512]{3,2,1,0:T(8,128)(2,1)S(1)}, u32[]{:S(2)}, u32[]{:S(2)}) %all-to-all-start) | async-done | bytes 2097184 | tf_op jit(solution)/shard_map/all_to_all | solution.py:74
  29.9 0.0 copy-start.1
  29.9 0.9 shard_map.85
  30.8 42.9 %all_to_all.15.arrived_ref = bf16[64,2,8,512]{3,2,1,0:T(8,128)(2,1)S(1)} all-to-all(bf16[64,2,8,512]{3,2,1,0:T(8,128)(2,1)S(1)} %bitcast.43), channel_id=1, replica_groups=mesh['dp'=4,'shard'=64] {'shard'}, dimensions={0} | all-to-all | bytes 2097152 | tf_op jit(solution)/shard_map/all_to_all | solution.py:89
  73.7 0.0 copy-done
  73.7 0.0 copy-done.1
  73.7 2.8 %shard_map.86 = bf16[64,2,8,512]{3,2,1,0:T(8,128)(2,1)} custom-call(bf16[64,2,8,512]{3,2,1,0:T(8,128)(2,1)S(1)} %all_to_all.15.arrived_ref, bf16[2,512,512]{2,1,0:T(8,128)(2,1)S(1)} %bitcast.44, bf16[2,512,512]{2,1,0:T(8,128)(2,1)S(1)} %bitcast.45), custom_call_target="tpu_custom_call" | custom-call | tf_op jit(solution)/shard_map/pallas_call | solution.py:92
  76.5 6.2 %all-to-all-start.2 = ((bf16[64,2,8,512]{3,2,1,0:T(8,128)(2,1)}), bf16[64,2,8,512]{3,2,1,0:T(8,128)(2,1)S(1)}, u32[]{:S(2)}, u32[]{:S(2)}) async-start(bf16[64,2,8,512]{3,2,1,0:T(8,128)(2,1)} %shard_map.86), calls=%async_computation.2 | async-start | bytes 2097152 | tf_op jit(solution)/shard_map/all_to_all | solution.py:100
  82.7 0.7 iota_compare_fusion.1
  83.4 0.0 copy-start.3
  83.4 3.9 %fusion.1 = f32[1,1,2,512,512]{4,3,2,1,0:T(8,128)} fusion(f32[1,1,2,512,512]{4,3,2,1,0:T(8,128)} %param.9, pred[2]{0:T(512)(128)(4,1)S(1)} %iota_compare_fusion.1, bf16[64,2,8,512]{3,2,1,0:T(8,128)(2,1)S(1)} %all_to_all.15.arrived_ref), kind=kOutput, calls=%fused_computation.3 | convolution fusion | flops 538968064 | bytes 5242882 | tf_op jit(solution)/shard_map/cji,cjk->cik/dot_general | solution.py:107
  87.3 0.0 copy-done.3
  87.3 2.3 %fusion.3 = f32[1,1,2,512,512]{4,3,2,1,0:T(8,128)} fusion(f32[1,1,2,512,512]{4,3,2,1,0:T(8,128)S(1)} %copy-done.3, pred[2]{0:T(512)(128)(4,1)S(1)} %iota_compare_fusion.1, bf16[64,2,8,512]{3,2,1,0:T(8,128)(2,1)S(1)} %all_to_all.15.arrived_ref), kind=kOutput, calls=%fused_computation.7 | convolution fusion | flops 538968064 | bytes 5242882 | tf_op jit(solution)/shard_map/cij,ckj->cik/dot_general | solution.py:106
  89.6 21.7 %all-to-all-done.2 = bf16[64,2,8,512]{3,2,1,0:T(8,128)(2,1)S(1)} async-done(((bf16[64,2,8,512]{3,2,1,0:T(8,128)(2,1)}), bf16[64,2,8,512]{3,2,1,0:T(8,128)(2,1)S(1)}, u32[]{:S(2)}, u32[]{:S(2)}) %all-to-all-start.2) | async-done | bytes 1048608 | tf_op jit(solution)/shard_map/all_to_all | solution.py:100
  111.3 1.4 %shard_map.87 = bf16[64,8,512]{2,1,0:T(8,128)(2,1)} custom-call(s32[64]{0:T(128)S(1)} %multiply_add_fusion.target_ref, bf16[128,8,512]{2,1,0:T(8,128)(2,1)S(1)} %bitcast.42), custom_call_target="tpu_custom_call" | custom-call | tf_op jit(solution)/shard_map/pallas_call | solution.py:110
  (1 shorter events, 0.0 us)
Async XLA Ops:
  0.6 4.9 %copy-start.2 = (s32[256,1]{0,1:T(1,128)S(1)}, s32[256,1]{0,1:T(1,128)}, u32[]{:S(2)}) copy-start(s32[256,1]{0,1:T(1,128)} %param.7) | copy-start | bytes 3076
  0.6 29.2 %all-to-all-start = ((bf16[4,64,8,512]{3,2,1,0:T(8,128)(2,1)}), bf16[4,64,8,512]{3,2,1,0:T(8,128)(2,1)S(1)}, u32[]{:S(2)}, u32[]{:S(2)}) async-start(bf16[4,64,8,512]{3,2,1,0:T(8,128)(2,1)} %bitcast.46), calls=%async_computation | async-start | bytes 4194304 | tf_op jit(solution)/shard_map/all_to_all | solution.py:74
  6.4 67.4 %copy-start = (bf16[1,1,2,512,512]{4,3,2,1,0:T(8,128)(2,1)S(1)}, bf16[1,1,2,512,512]{4,3,2,1,0:T(8,128)(2,1)}, u32[]{:S(2)}) copy-start(bf16[1,1,2,512,512]{4,3,2,1,0:T(8,128)(2,1)} %param.10) | copy-start | bytes 3145732
  29.9 43.9 %copy-start.1 = (bf16[1,1,2,512,512]{4,3,2,1,0:T(8,128)(2,1)S(1)}, bf16[1,1,2,512,512]{4,3,2,1,0:T(8,128)(2,1)}, u32[]{:S(2)}) copy-start(bf16[1,1,2,512,512]{4,3,2,1,0:T(8,128)(2,1)} %param.11) | copy-start | bytes 3145732
  76.5 34.7 %all-to-all-start.2 = ((bf16[64,2,8,512]{3,2,1,0:T(8,128)(2,1)}), bf16[64,2,8,512]{3,2,1,0:T(8,128)(2,1)S(1)}, u32[]{:S(2)}, u32[]{:S(2)}) async-start(bf16[64,2,8,512]{3,2,1,0:T(8,128)(2,1)} %shard_map.86), calls=%async_computation.2 | async-start | bytes 2097152 | tf_op jit(solution)/shard_map/all_to_all | solution.py:100
  83.4 4.0 %copy-start.3 = (f32[1,1,2,512,512]{4,3,2,1,0:T(8,128)S(1)}, f32[1,1,2,512,512]{4,3,2,1,0:T(8,128)}, u32[]{:S(2)}) copy-start(f32[1,1,2,512,512]{4,3,2,1,0:T(8,128)} %param.8) | copy-start | bytes 6291460

commit v2 on v1

--- a/solution.py
+++ b/solution.py
@@ -1,3 +1,5 @@
+import functools
+
 import jax
 import jax.numpy as jnp
 from jax import lax
@@ -10,18 +12,55 @@
 VMEM_LIMIT = 48 * 1024 * 1024
 
 
-def mean_and_route(target_ref, parts_ref, out_ref):
-    replicas, group = parts_ref.shape[:2]
+def half_of(grads_ref, replicas, ahead, high):
+    group = grads_ref.shape[0] // replicas
+    start = lax.rem(lax.axis_index("dp") + ahead, replicas) * group + high * (group // 2)
+    return grads_ref.at[pl.ds(start, group // 2)]
+
+
+def stage_sends(replicas, grads_ref, far_low, far_high, near_right, near_left, sems):
+    wanted = ((2, 0, far_low), (2, 1, far_high), (1, 1, near_right), (replicas - 1, 0, near_left))
+    copies = [
+        pltpu.make_async_copy(half_of(grads_ref, replicas, ahead, high), out, sems.at[k])
+        for k, (ahead, high, out) in enumerate(wanted)
+    ]
+    for copy in copies:
+        copy.start()
+    for copy in copies:
+        copy.wait()
+
+
+def partial_sums(replicas, grads_ref, low_ref, high_ref, right_ref, left_ref, own_low, own_high, sems):
+    half = low_ref.shape[0]
+    copies = [
+        pltpu.make_async_copy(half_of(grads_ref, replicas, 1, 0), own_low, sems.at[0]),
+        pltpu.make_async_copy(half_of(grads_ref, replicas, replicas - 1, 1), own_high, sems.at[1]),
+    ]
+    for copy in copies:
+        copy.start()
+    for copy in copies:
+        copy.wait()
+
+    def one(b, _):
+        right_ref[b] = (own_low[b].astype(jnp.float32) + low_ref[b].astype(jnp.float32)).astype(jnp.bfloat16)
+        left_ref[b] = (own_high[b].astype(jnp.float32) + high_ref[b].astype(jnp.float32)).astype(jnp.bfloat16)
+        return 0
+
+    lax.fori_loop(0, half, one, 0, unroll=8)
+
+
+def mean_and_route(replicas, target_ref, own_ref, ll_ref, lh_ref, rl_ref, rh_ref, out_ref):
+    half = ll_ref.shape[0]
     out_ref[...] = jnp.zeros_like(out_ref)
 
     def one(b, _):
-        total = parts_ref[0, b].astype(jnp.float32)
-        for r in range(1, replicas):
-            total = total + parts_ref[r, b].astype(jnp.float32)
-        out_ref[target_ref[b]] = (total / replicas).astype(jnp.bfloat16)
+        low = own_ref[b].astype(jnp.float32) + ll_ref[b].astype(jnp.float32) + rl_ref[b].astype(jnp.float32)
+        out_ref[target_ref[b]] = (low / replicas).astype(jnp.bfloat16)
+        high = own_ref[b + half].astype(jnp.float32) + lh_ref[b].astype(jnp.float32) + rh_ref[b].astype(jnp.float32)
+        out_ref[target_ref[b + half]] = (high / replicas).astype(jnp.bfloat16)
         return 0
 
-    lax.fori_loop(0, group, one, 0, unroll=8)
+    lax.fori_loop(0, half, one, 0, unroll=4)
 
 
 def precondition(arrived_ref, lroot_ref, rroot_ref, out_ref, block):
@@ -60,6 +99,10 @@
     return pl.BlockSpec(memory_space=pltpu.SMEM)
 
 
+def in_hbm():
+    return pl.BlockSpec(memory_space=pltpu.HBM)
+
+
 def params():
     return pltpu.CompilerParams(vmem_limit_bytes=VMEM_LIMIT)
 
@@ -71,21 +114,47 @@
     width = grads.shape[3]
     group = grads.shape[1] // replicas
     slots_each = left_factor.shape[2]
-    parts = lax.all_to_all(
-        grads[0].reshape(replicas, group, rows, width), "dp", split_axis=0, concat_axis=0, tiled=True
-    )
+    me = lax.axis_index("dp")
+    half = group // 2
+    rightward = [(k, (k + 1) % replicas) for k in range(replicas)]
+    leftward = [(k, (k - 1) % replicas) for k in range(replicas)]
+    in_place = pltpu.with_memory_space_constraint(grads[0], pltpu.HBM)
+    piece = jax.ShapeDtypeStruct((half, rows, width), jnp.bfloat16)
+    far_low, far_high, near_right, near_left = pl.pallas_call(
+        functools.partial(stage_sends, replicas),
+        out_shape=[piece] * 4,
+        in_specs=[in_hbm()],
+        out_specs=[in_vmem()] * 4,
+        scratch_shapes=[pltpu.SemaphoreType.DMA((4,))],
+        compiler_params=params(),
+    )(in_place)
+    low = lax.ppermute(far_low, "dp", rightward)
+    high = lax.ppermute(far_high, "dp", leftward)
+    from_left_high = lax.ppermute(near_right, "dp", rightward)
+    from_right_low = lax.ppermute(near_left, "dp", leftward)
+    to_right, to_left = pl.pallas_call(
+        functools.partial(partial_sums, replicas),
+        out_shape=[piece] * 2,
+        in_specs=[in_hbm(), in_vmem(), in_vmem()],
+        out_specs=[in_vmem()] * 2,
+        scratch_shapes=[pltpu.VMEM(piece.shape, piece.dtype)] * 2 + [pltpu.SemaphoreType.DMA((2,))],
+        compiler_params=params(),
+    )(in_place, low, high)
+    from_left_low = lax.ppermute(to_right, "dp", rightward)
+    from_right_high = lax.ppermute(to_left, "dp", leftward)
+    own = lax.dynamic_slice_in_dim(grads[0], me * group, group)
     table = lax.dynamic_slice_in_dim(owner[:, 0], lax.axis_index("dp") * group, group)
     index = jnp.arange(group, dtype=jnp.int32)
     same = (table[:, None] == table[None, :]) & (index[None, :] < index[:, None])
     slots = jnp.sum(same.astype(jnp.int32), axis=1)
     target = table * slots_each + slots
     outgoing = pl.pallas_call(
-        mean_and_route,
+        functools.partial(mean_and_route, replicas),
         out_shape=jax.ShapeDtypeStruct((owners * slots_each, rows, width), jnp.bfloat16),
-        in_specs=[in_smem(), in_vmem()],
+        in_specs=[in_smem()] + [in_vmem()] * 5,
         out_specs=in_vmem(),
         compiler_params=params(),
-    )(target, parts)
+    )(target, own, from_left_low, from_left_high, from_right_low, from_right_high)
     arrived = lax.all_to_all(
         outgoing.reshape(owners, slots_each, rows, width), "shard", split_axis=0, concat_axis=0, tiled=True
     )

time: 113 us -> 104 us (0.920)
  waiting for transfers between devices: 45.1 us -> 29 us
  starting transfers between devices: 11 us -> 15.1 us
  Pallas kernels: 5.16 us -> 7.48 us
    all_to_all x1 -> x0, waiting for transfers between devices: 23.5 us -> none  [shards(): lax.all_to_all(grads[0].reshape(replicas, group, rows, width), 'dp', spli...]
    ppermute x0 -> x6, starting transfers between devices: none -> 8.91 us  [the longest x1 2.57 us: shards(): from_right_low = lax.ppermute(near_left, 'dp', leftward)]
    ppermute x0 -> x6, waiting for transfers between devices: none -> 7.34 us  [the longest x1 4.14 us: shards(): from_left_low = lax.ppermute(to_right, 'dp', rightward)]
    all_to_all x1 -> x0, starting transfers between devices: 4.85 us -> none  [shards(): lax.all_to_all(grads[0].reshape(replicas, group, rows, width), 'dp', spli...]
    pallas_call x1 -> x3, Pallas kernels: 0.94 us -> 3.28 us  [the longest x1 1.24 us: shards(): pl.pallas_call(functools.partial(stage_sends, replicas), out_shape=[piece...]
  transfers between devices with their start and end apart: 2 -> 7, of which waited for: 2 -> 5; matrix products, arithmetic and copies ran while one was open for 7% -> 9% of each run, Pallas kernels for 0% -> 1%
where the time goes in v2:
time: 104 us
  blocking collectives  42.6 us (41%)
  waiting for transfers between devices  29 us (28%)
  starting transfers between devices  15.1 us (15%)
  Pallas kernels  7.48 us (7%)
  matrix products  6.22 us (6%)
  other arithmetic  1.53 us (1%)
  local copies, waits for them, and re-layouts  1.1 us (1%)
    all_to_all x1, blocking collectives, shards(): lax.all_to_all(outgoing.reshape(owners, slots_each, rows, width), 'shard'...  42.6 us
    all_to_all x1, waiting for transfers between devices, shards(): lax.all_to_all(finished, 'shard', split_axis=0, concat_axis=0, tiled=True)  21.7 us
    all_to_all x1, starting transfers between devices, shards(): lax.all_to_all(finished, 'shard', split_axis=0, concat_axis=0, tiled=True)  6.19 us
    ppermute x1, waiting for transfers between devices, shards(): from_left_low = lax.ppermute(to_right, 'dp', rightward)  4.14 us
    dot_general x1, matrix products, shards(): jnp.einsum('cji,cjk->cik', blocks, blocks, preferred_element_type=jnp.flo...  3.93 us
    pallas_call x1, Pallas kernels, shards(): pl.pallas_call(precondition, out_shape=jax.ShapeDtypeStruct((owners, slot...  2.76 us
    ppermute x1, starting transfers between devices, shards(): from_right_low = lax.ppermute(near_left, 'dp', leftward)  2.57 us
    dot_general x1, matrix products, shards(): jnp.einsum('cij,ckj->cik', blocks, blocks, preferred_element_type=jnp.flo...  2.29 us
  transfers between devices with their start and end apart: 7, of which 5 were waited for; matrix products, arithmetic and copies ran while one was open for 9% of the time, Pallas kernels for 1%

profile of v2, /device:TPU:1, one launch (start us, length us, event | category | flops | bytes accessed | tf_op | source)
XLA Modules:
  0.0 103.8 jit_solution(15075973549781542241)
XLA Ops:
  0.6 1.2 %shard_map.85 = (bf16[32,8,512]{2,1,0:T(8,128)(2,1)S(1)}, bf16[32,8,512]{2,1,0:T(8,128)(2,1)S(1)}, bf16[32,8,512]{2,1,0:T(8,128)(2,1)S(1)}, bf16[32,8,512]{2,1,0:T(8,128)(2,1)S(1)}) custom-call(bf16[256,8,512]{2,1,0:T(8,128)(2,1)} %bitcast.48), custom_call_target="tpu_custom_call" | custom-call | tf_op jit(solution)/shard_map/pallas_call | solution.py:123
  1.9 2.1 %collective-permute-start = (bf16[32,8,512]{2,1,0:T(8,128)(2,1)S(1)}, bf16[32,8,512]{2,1,0:T(8,128)(2,1)S(1)}, u32[]{:S(2)}, u32[]{:S(2)}) collective-permute-start(bf16[32,8,512]{2,1,0:T(8,128)(2,1)S(1)} %get-tuple-element.9), channel_id=1, source_target_pairs={{0,64},{64,128},{128,192},{192,0},{1,65},{65,129},{129,193},{193,1... | collective-permute-start | bytes 786440 | tf_op jit(solution)/shard_map/ppermute | solution.py:131
  4.0 1.4 %collective-permute-start.1 = (bf16[32,8,512]{2,1,0:T(8,128)(2,1)S(1)}, bf16[32,8,512]{2,1,0:T(8,128)(2,1)S(1)}, u32[]{:S(2)}, u32[]{:S(2)}) collective-permute-start(bf16[32,8,512]{2,1,0:T(8,128)(2,1)S(1)} %get-tuple-element.10), channel_id=1, source_target_pairs={{0,192},{64,0},{128,64},{192,128},{1,193},{65,1},{129,65},{193,129... | collective-permute-start | bytes 786440 | tf_op jit(solution)/shard_map/ppermute | solution.py:132
  5.4 0.1 collective-permute-start.3
  5.5 2.6 %collective-permute-start.4 = (bf16[32,8,512]{2,1,0:T(8,128)(2,1)S(1)}, bf16[32,8,512]{2,1,0:T(8,128)(2,1)S(1)}, u32[]{:S(2)}, u32[]{:S(2)}) collective-permute-start(bf16[32,8,512]{2,1,0:T(8,128)(2,1)S(1)} %get-tuple-element.13), channel_id=1, source_target_pairs={{0,192},{64,0},{128,64},{192,128},{1,193},{65,1},{129,65},{193,129... | collective-permute-start | bytes 786440 | tf_op jit(solution)/shard_map/ppermute | solution.py:134
  8.0 0.7 fusion.9
  8.7 1.1 %dynamic-slice_bitcast_fusion.own_ref = bf16[64,8,512]{2,1,0:T(8,128)(2,1)S(1)} fusion(bf16[1,256,8,512]{3,2,1,0:T(8,128)(2,1)} %param.6, s32[]{:T(128)S(6)} %select_n.11), kind=kLoop, calls=%fused_computation.12 | loop fusion | bytes 1048580 | tf_op jit(solution)/shard_map/dynamic_slice | solution.py:145
  9.8 0.7 collective-permute-done.1.high_ref
  10.5 1.2 %shard_map.86 = (bf16[32,8,512]{2,1,0:T(8,128)(2,1)S(1)}, bf16[32,8,512]{2,1,0:T(8,128)(2,1)S(1)}) custom-call(bf16[256,8,512]{2,1,0:T(8,128)(2,1)} %bitcast.49, bf16[32,8,512]{2,1,0:T(8,128)(2,1)S(1)} %collective-permute-done.low_ref, bf16[32,8,512]{2,1,0:T(8,128)(2,1)S(1)} %collective-permute-done.1.high_ref), custom_call_target="tpu_custom_call" | custom-call | tf_op jit(solution)/shard_map/pallas_call | solution.py:135
  11.7 1.6 %collective-permute-start.2 = (bf16[32,8,512]{2,1,0:T(8,128)(2,1)S(1)}, bf16[32,8,512]{2,1,0:T(8,128)(2,1)S(1)}, u32[]{:S(2)}, u32[]{:S(2)}) collective-permute-start(bf16[32,8,512]{2,1,0:T(8,128)(2,1)S(1)} %get-tuple-element.11), channel_id=1, source_target_pairs={{0,64},{64,128},{128,192},{192,0},{1,65},{65,129},{129,193},{193,1... | collective-permute-start | bytes 786440 | tf_op jit(solution)/shard_map/ppermute | solution.py:143
  13.3 1.1 %collective-permute-start.5 = (bf16[32,8,512]{2,1,0:T(8,128)(2,1)S(1)}, bf16[32,8,512]{2,1,0:T(8,128)(2,1)S(1)}, u32[]{:S(2)}, u32[]{:S(2)}) collective-permute-start(bf16[32,8,512]{2,1,0:T(8,128)(2,1)S(1)} %get-tuple-element.14), channel_id=1, source_target_pairs={{0,192},{64,0},{128,64},{192,128},{1,193},{65,1},{129,65},{193,129... | collective-permute-start | bytes 786440 | tf_op jit(solution)/shard_map/ppermute | solution.py:144
  14.4 0.2 convert_reduce_fusion
  14.7 1.5 %collective-permute-done.4.rl_ref = bf16[32,8,512]{2,1,0:T(8,128)(2,1)S(1)} collective-permute-done((bf16[32,8,512]{2,1,0:T(8,128)(2,1)S(1)}, bf16[32,8,512]{2,1,0:T(8,128)(2,1)S(1)}, u32[]{:S(2)}, u32[]{:S(2)}) %collective-permute-start.4) | collective-permute-done | bytes 262176 | tf_op jit(solution)/shard_map/ppermute | solution.py:134
  16.1 4.1 %collective-permute-done.2.ll_ref = bf16[32,8,512]{2,1,0:T(8,128)(2,1)S(1)} collective-permute-done((bf16[32,8,512]{2,1,0:T(8,128)(2,1)S(1)}, bf16[32,8,512]{2,1,0:T(8,128)(2,1)S(1)}, u32[]{:S(2)}, u32[]{:S(2)}) %collective-permute-start.2) | collective-permute-done | bytes 262176 | tf_op jit(solution)/shard_map/ppermute | solution.py:143
  20.3 1.1 %collective-permute-done.5.rh_ref = bf16[32,8,512]{2,1,0:T(8,128)(2,1)S(1)} collective-permute-done((bf16[32,8,512]{2,1,0:T(8,128)(2,1)S(1)}, bf16[32,8,512]{2,1,0:T(8,128)(2,1)S(1)}, u32[]{:S(2)}, u32[]{:S(2)}) %collective-permute-start.5) | collective-permute-done | bytes 262176 | tf_op jit(solution)/shard_map/ppermute | solution.py:144
  21.3 0.9 shard_map.87
  22.2 42.6 %all_to_all.10.arrived_ref = bf16[64,2,8,512]{3,2,1,0:T(8,128)(2,1)S(1)} all-to-all(bf16[64,2,8,512]{3,2,1,0:T(8,128)(2,1)S(1)} %bitcast.45), channel_id=1, replica_groups=mesh['dp'=4,'shard'=64] {'shard'}, dimensions={0} | all-to-all | bytes 2097152 | tf_op jit(solution)/shard_map/all_to_all | solution.py:158
  64.8 2.8 %shard_map.88 = bf16[64,2,8,512]{3,2,1,0:T(8,128)(2,1)} custom-call(bf16[64,2,8,512]{3,2,1,0:T(8,128)(2,1)S(1)} %all_to_all.10.arrived_ref, bf16[2,512,512]{2,1,0:T(8,128)(2,1)S(1)} %bitcast.46, bf16[2,512,512]{2,1,0:T(8,128)(2,1)S(1)} %bitcast.47), custom_call_target="tpu_custom_call" | custom-call | tf_op jit(solution)/shard_map/pallas_call | solution.py:161
  67.6 6.2 %all-to-all-start.1 = ((bf16[64,2,8,512]{3,2,1,0:T(8,128)(2,1)}), bf16[64,2,8,512]{3,2,1,0:T(8,128)(2,1)S(1)}, u32[]{:S(2)}, u32[]{:S(2)}) async-start(bf16[64,2,8,512]{3,2,1,0:T(8,128)(2,1)} %shard_map.88), calls=%async_computation.1 | async-start | bytes 2097152 | tf_op jit(solution)/shard_map/all_to_all | solution.py:169
  73.8 0.7 iota_compare_fusion.1
  74.5 3.9 %fusion.1 = f32[1,1,2,512,512]{4,3,2,1,0:T(8,128)} fusion(f32[1,1,2,512,512]{4,3,2,1,0:T(8,128)} %param.9, pred[2]{0:T(512)(128)(4,1)S(1)} %iota_compare_fusion.1, bf16[64,2,8,512]{3,2,1,0:T(8,128)(2,1)S(1)} %all_to_all.10.arrived_ref), kind=kOutput, calls=%fused_computation.3 | convolution fusion | flops 538968064 | bytes 5242882 | tf_op jit(solution)/shard_map/cji,cjk->cik/dot_general | solution.py:176
  78.4 2.3 %fusion.3 = f32[1,1,2,512,512]{4,3,2,1,0:T(8,128)} fusion(f32[1,1,2,512,512]{4,3,2,1,0:T(8,128)S(1)} %copy-done.3, pred[2]{0:T(512)(128)(4,1)S(1)} %iota_compare_fusion.1, bf16[64,2,8,512]{3,2,1,0:T(8,128)(2,1)S(1)} %all_to_all.10.arrived_ref), kind=kOutput, calls=%fused_computation.7 | convolution fusion | flops 538968064 | bytes 5242882 | tf_op jit(solution)/shard_map/cij,ckj->cik/dot_general | solution.py:175
  80.7 21.7 %all-to-all-done.1 = bf16[64,2,8,512]{3,2,1,0:T(8,128)(2,1)S(1)} async-done(((bf16[64,2,8,512]{3,2,1,0:T(8,128)(2,1)}), bf16[64,2,8,512]{3,2,1,0:T(8,128)(2,1)S(1)}, u32[]{:S(2)}, u32[]{:S(2)}) %all-to-all-start.1) | async-done | bytes 1048608 | tf_op jit(solution)/shard_map/all_to_all | solution.py:169
  102.4 1.4 %shard_map.89 = bf16[64,8,512]{2,1,0:T(8,128)(2,1)} custom-call(s32[64]{0:T(128)S(1)} %multiply_add_fusion.target_ref, bf16[128,8,512]{2,1,0:T(8,128)(2,1)S(1)} %bitcast.44), custom_call_target="tpu_custom_call" | custom-call | tf_op jit(solution)/shard_map/pallas_call | solution.py:179
  (11 shorter events, 0.0 us)
Async XLA Ops:
  0.6 7.4 %copy-start.2 = (s32[256,1]{0,1:T(1,128)S(1)}, s32[256,1]{0,1:T(1,128)}, u32[]{:S(2)}) copy-start(s32[256,1]{0,1:T(1,128)} %param.7) | copy-start | bytes 3076
  1.9 7.9 %collective-permute-start = (bf16[32,8,512]{2,1,0:T(8,128)(2,1)S(1)}, bf16[32,8,512]{2,1,0:T(8,128)(2,1)S(1)}, u32[]{:S(2)}, u32[]{:S(2)}) collective-permute-start(bf16[32,8,512]{2,1,0:T(8,128)(2,1)S(1)} %get-tuple-element.9), channel_id=1, source_target_pairs={{0,64},{64,128},{128,192},{192,0},{1,65},{65,129},{129,193},{193,1... | collective-permute-start | bytes 786440 | tf_op jit(solution)/shard_map/ppermute | solution.py:131
  4.0 6.5 %collective-permute-start.1 = (bf16[32,8,512]{2,1,0:T(8,128)(2,1)S(1)}, bf16[32,8,512]{2,1,0:T(8,128)(2,1)S(1)}, u32[]{:S(2)}, u32[]{:S(2)}) collective-permute-start(bf16[32,8,512]{2,1,0:T(8,128)(2,1)S(1)} %get-tuple-element.10), channel_id=1, source_target_pairs={{0,192},{64,0},{128,64},{192,128},{1,193},{65,1},{129,65},{193,129... | collective-permute-start | bytes 786440 | tf_op jit(solution)/shard_map/ppermute | solution.py:132
  5.4 9.3 %collective-permute-start.3 = (bf16[32,8,512]{2,1,0:T(8,128)(2,1)S(1)}, bf16[32,8,512]{2,1,0:T(8,128)(2,1)S(1)}, u32[]{:S(2)}, u32[]{:S(2)}) collective-permute-start(bf16[32,8,512]{2,1,0:T(8,128)(2,1)S(1)} %get-tuple-element.12), channel_id=1, source_target_pairs={{0,64},{64,128},{128,192},{192,0},{1,65},{65,129},{129,193},{193,1... | collective-permute-start | bytes 786440 | tf_op jit(solution)/shard_map/ppermute | solution.py:133
  5.5 10.7 %collective-permute-start.4 = (bf16[32,8,512]{2,1,0:T(8,128)(2,1)S(1)}, bf16[32,8,512]{2,1,0:T(8,128)(2,1)S(1)}, u32[]{:S(2)}, u32[]{:S(2)}) collective-permute-start(bf16[32,8,512]{2,1,0:T(8,128)(2,1)S(1)} %get-tuple-element.13), channel_id=1, source_target_pairs={{0,192},{64,0},{128,64},{192,128},{1,193},{65,1},{129,65},{193,129... | collective-permute-start | bytes 786440 | tf_op jit(solution)/shard_map/ppermute | solution.py:134
  11.7 8.6 %collective-permute-start.2 = (bf16[32,8,512]{2,1,0:T(8,128)(2,1)S(1)}, bf16[32,8,512]{2,1,0:T(8,128)(2,1)S(1)}, u32[]{:S(2)}, u32[]{:S(2)}) collective-permute-start(bf16[32,8,512]{2,1,0:T(8,128)(2,1)S(1)} %get-tuple-element.11), channel_id=1, source_target_pairs={{0,64},{64,128},{128,192},{192,0},{1,65},{65,129},{129,193},{193,1... | collective-permute-start | bytes 786440 | tf_op jit(solution)/shard_map/ppermute | solution.py:143
  13.3 8.0 %collective-permute-start.5 = (bf16[32,8,512]{2,1,0:T(8,128)(2,1)S(1)}, bf16[32,8,512]{2,1,0:T(8,128)(2,1)S(1)}, u32[]{:S(2)}, u32[]{:S(2)}) collective-permute-start(bf16[32,8,512]{2,1,0:T(8,128)(2,1)S(1)} %get-tuple-element.14), channel_id=1, source_target_pairs={{0,192},{64,0},{128,64},{192,128},{1,193},{65,1},{129,65},{193,129... | collective-permute-start | bytes 786440 | tf_op jit(solution)/shard_map/ppermute | solution.py:144
  14.6 50.2 %copy-start = (bf16[1,1,2,512,512]{4,3,2,1,0:T(8,128)(2,1)S(1)}, bf16[1,1,2,512,512]{4,3,2,1,0:T(8,128)(2,1)}, u32[]{:S(2)}) copy-start(bf16[1,1,2,512,512]{4,3,2,1,0:T(8,128)(2,1)} %param.10) | copy-start | bytes 3145732
  14.6 50.2 %copy-start.1 = (bf16[1,1,2,512,512]{4,3,2,1,0:T(8,128)(2,1)S(1)}, bf16[1,1,2,512,512]{4,3,2,1,0:T(8,128)(2,1)}, u32[]{:S(2)}) copy-start(bf16[1,1,2,512,512]{4,3,2,1,0:T(8,128)(2,1)} %param.11) | copy-start | bytes 3145732
  67.6 34.7 %all-to-all-start.1 = ((bf16[64,2,8,512]{3,2,1,0:T(8,128)(2,1)}), bf16[64,2,8,512]{3,2,1,0:T(8,128)(2,1)S(1)}, u32[]{:S(2)}, u32[]{:S(2)}) async-start(bf16[64,2,8,512]{3,2,1,0:T(8,128)(2,1)} %shard_map.88), calls=%async_computation.1 | async-start | bytes 2097152 | tf_op jit(solution)/shard_map/all_to_all | solution.py:169
  74.5 3.9 %copy-start.3 = (f32[1,1,2,512,512]{4,3,2,1,0:T(8,128)S(1)}, f32[1,1,2,512,512]{4,3,2,1,0:T(8,128)}, u32[]{:S(2)}) copy-start(f32[1,1,2,512,512]{4,3,2,1,0:T(8,128)} %param.8) | copy-start | bytes 6291460

commit v3 on v2

v3 whole, which is shorter than its diff:
```python
import functools

import jax
import jax.numpy as jnp
from jax import lax
from jax.experimental import pallas as pl
from jax.experimental.pallas import tpu as pltpu
from jax.sharding import PartitionSpec as P

BETA = 0.95
EPS = 1e-06
VMEM_LIMIT = 16 * 1024 * 1024


def half_of(grads_ref, replicas, ahead, high):
    group = grads_ref.shape[0] // replicas
    start = lax.rem(lax.axis_index("dp") + ahead, replicas) * group + high * (group // 2)
    return grads_ref.at[pl.ds(start, group // 2)]


def stage(replicas, wanted, grads_ref, *refs):
    outs, sems = refs[:-1], refs[-1]
    copies = [
        pltpu.make_async_copy(half_of(grads_ref, replicas, ahead, high), out, sems.at[k])
        for k, ((ahead, high), out) in enumerate(zip(wanted, outs))
    ]
    for copy in copies:
        copy.start()
    for copy in copies:
        copy.wait()


def partial_sums(own_low, own_high, low_ref, high_ref, right_ref, left_ref):
    half = low_ref.shape[0]

    def one(b, _):
        right_ref[b] = (own_low[b].astype(jnp.float32) + low_ref[b].astype(jnp.float32)).astype(jnp.bfloat16)
        left_ref[b] = (own_high[b].astype(jnp.float32) + high_ref[b].astype(jnp.float32)).astype(jnp.bfloat16)
        return 0

    lax.fori_loop(0, half, one, 0, unroll=8)


def mean_and_route(replicas, target_ref, own_ref, ll_ref, lh_ref, rl_ref, rh_ref, out_ref):
    half = ll_ref.shape[0]
    out_ref[...] = jnp.zeros_like(out_ref)

    def one(b, _):
        low = own_ref[b].astype(jnp.float32) + ll_ref[b].astype(jnp.float32) + rl_ref[b].astype(jnp.float32)
        out_ref[target_ref[b]] = (low / replicas).astype(jnp.bfloat16)
        high = own_ref[b + half].astype(jnp.float32) + lh_ref[b].astype(jnp.float32) + rh_ref[b].astype(jnp.float32)
        out_ref[target_ref[b + half]] = (high / replicas).astype(jnp.bfloat16)
        return 0

    lax.fori_loop(0, half, one, 0, unroll=4)


def precondition(arrived_ref, lroot_ref, rroot_ref, out_ref, block):
    senders, slots, rows, width = arrived_ref.shape
    entries = senders * rows * width
    for c in range(slots):
        power = jnp.zeros((rows, width), jnp.float32)
        for s in range(0, senders, 2):
            first = arrived_ref[s, c].astype(jnp.float32)
            second = arrived_ref[s + 1, c].astype(jnp.float32)
            power = power + (first * first + second * second)
            block[c, pl.ds(s * rows, 2 * rows), :] = jnp.concatenate([first, second], axis=0).astype(jnp.bfloat16)
        half = jnp.dot(lroot_ref[c], block[c], preferred_element_type=jnp.float32).astype(jnp.bfloat16)
        pre = jnp.dot(half, rroot_ref[c], preferred_element_type=jnp.float32)
        grad_power = jnp.sum(power, keepdims=True)
        pre_power = jnp.sum(pre * pre, keepdims=True)
        ratio = jnp.sqrt(grad_power / entries + EPS) / jnp.sqrt(pre_power / entries + EPS)
        for s in range(senders):
            out_ref[s, c] = (pre[s * rows : (s + 1) * rows] * ratio).astype(jnp.bfloat16)


def factors(count_ref, arrived_ref, left_ref, right_ref, new_left_ref, new_right_ref, block):
    senders, _, rows, _ = arrived_ref.shape
    c = pl.program_id(0)
    for s in range(0, senders, 2):
        pair = [arrived_ref[s + k, c].astype(jnp.float32) for k in range(2)]
        block[pl.ds(s * rows, 2 * rows), :] = jnp.concatenate(pair, axis=0).astype(jnp.bfloat16)
    filled = c < count_ref[0]
    for axis, old_ref, new_ref in ((1, left_ref, new_left_ref), (0, right_ref, new_right_ref)):
        gram = lax.dot_general(
            block[...], block[...], (((axis,), (axis,)), ((), ())), preferred_element_type=jnp.float32
        )
        old = old_ref[0]
        new_ref[0] = jnp.where(filled, BETA * old + (1.0 - BETA) * gram, old)


def pick(parts, target_ref, returned_ref, out_ref, rows_of, sems):
    each = rows_of.shape[0] // parts
    copies = []
    for k in range(parts):
        span = pl.ds(k * each, each)
        for b in range(k * each, (k + 1) * each):
            rows_of[b] = returned_ref[target_ref[b]]
        copies.append(pltpu.make_async_copy(rows_of.at[span], out_ref.at[span], sems.at[k]))
        copies[-1].start()
    for copy in copies:
        copy.wait()


def in_vmem():
    return pl.BlockSpec(memory_space=pltpu.VMEM)


def in_smem():
    return pl.BlockSpec(memory_space=pltpu.SMEM)


def in_hbm():
    return pl.BlockSpec(memory_space=pltpu.HBM)


def params():
    return pltpu.CompilerParams(vmem_limit_bytes=VMEM_LIMIT)


def shards(grads, owner, left_factor, right_factor, left_root, right_root):
    replicas = lax.axis_size("dp")
    owners = lax.axis_size("shard")
    rows = grads.shape[2]
    width = grads.shape[3]
    group = grads.shape[1] // replicas
    slots_each = left_factor.shape[2]
    me = lax.axis_index("dp")
    half = group // 2
    rightward = [(k, (k + 1) % replicas) for k in range(replicas)]
    leftward = [(k, (k - 1) % replicas) for k in range(replicas)]
    in_place = pltpu.with_memory_space_constraint(grads[0], pltpu.HBM)
    piece = jax.ShapeDtypeStruct((half, rows, width), jnp.bfloat16)

    def staged(wanted):
        return pl.pallas_call(
            functools.partial(stage, replicas, wanted),
            out_shape=[piece] * len(wanted),
            in_specs=[in_hbm()],
            out_specs=[in_vmem()] * len(wanted),
            scratch_shapes=[pltpu.SemaphoreType.DMA((len(wanted),))],
            compiler_params=params(),
        )(in_place)

    far_low, far_high = staged(((2, 0), (2, 1)))
    near_right, near_left, own_low, own_high = staged(((1, 1), (replicas - 1, 0), (1, 0), (replicas - 1, 1)))
    low = lax.ppermute(far_low, "dp", rightward)
    high = lax.ppermute(far_high, "dp", leftward)
    from_left_high = lax.ppermute(near_right, "dp", rightward)
    from_right_low = lax.ppermute(near_left, "dp", leftward)
    to_right, to_left = pl.pallas_call(
        partial_sums,
        out_shape=[piece] * 2,
        in_specs=[in_vmem()] * 4,
        out_specs=[in_vmem()] * 2,
        compiler_params=params(),
    )(own_low, own_high, low, high)
    from_left_low = lax.ppermute(to_right, "dp", rightward)
    from_right_high = lax.ppermute(to_left, "dp", leftward)
    own = lax.dynamic_slice_in_dim(grads[0], me * group, group)
    table = lax.dynamic_slice_in_dim(owner[:, 0], lax.axis_index("dp") * group, group)
    index = jnp.arange(group, dtype=jnp.int32)
    same = (table[:, None] == table[None, :]) & (index[None, :] < index[:, None])
    slots = jnp.sum(same.astype(jnp.int32), axis=1)
    target = table * slots_each + slots
    target = pltpu.with_memory_space_constraint(target, pltpu.SMEM)
    outgoing = pl.pallas_call(
        functools.partial(mean_and_route, replicas),
        out_shape=jax.ShapeDtypeStruct((owners * slots_each, rows, width), jnp.bfloat16),
        in_specs=[in_smem()] + [in_vmem()] * 5,
        out_specs=in_vmem(),
        compiler_params=params(),
    )(target, own, from_left_low, from_left_high, from_right_low, from_right_high)
    arrived = lax.all_to_all(
        outgoing.reshape(owners, slots_each, rows, width), "shard", split_axis=0, concat_axis=0, tiled=True
    )
    finished = pl.pallas_call(
        precondition,
        out_shape=jax.ShapeDtypeStruct((owners, slots_each, rows, width), jnp.bfloat16),
        in_specs=[in_vmem()] * 3,
        out_specs=in_vmem(),
        scratch_shapes=[pltpu.VMEM((slots_each, owners * rows, width), jnp.bfloat16)],
        compiler_params=params(),
    )(arrived, left_root[0, 0], right_root[0, 0])
    returned = lax.all_to_all(finished, "shard", split_axis=0, concat_axis=0, tiled=True)
    count = jnp.sum((table == lax.axis_index("shard")).astype(jnp.int32)).reshape(1)
    order = left_factor.shape[3:]
    of_slot = pl.BlockSpec((1, *order), lambda c: (c, 0, 0))
    new_left, new_right = pl.pallas_call(
        factors,
        grid=(slots_each,),
        out_shape=[jax.ShapeDtypeStruct((slots_each, *order), jnp.float32)] * 2,
        in_specs=[in_smem(), in_vmem(), of_slot, of_slot],
        out_specs=[of_slot] * 2,
        scratch_shapes=[pltpu.VMEM(order, jnp.bfloat16)],
        compiler_params=params(),
        cost_estimate=pl.CostEstimate(
            flops=8 * slots_each * order[0] ** 3, bytes_accessed=18 * slots_each * order[0] ** 2, transcendentals=0
        ),
    )(
        count,
        arrived,
        pltpu.with_memory_space_constraint(left_factor[0, 0], pltpu.HBM),
        pltpu.with_memory_space_constraint(right_factor[0, 0], pltpu.HBM),
    )
    update = pl.pallas_call(
        functools.partial(pick, 4),
        out_shape=jax.ShapeDtypeStruct((group, rows, width), jnp.bfloat16),
        in_specs=[in_smem(), in_vmem()],
        out_specs=in_hbm(),
        scratch_shapes=[pltpu.VMEM((group, rows, width), jnp.bfloat16), pltpu.SemaphoreType.DMA((4,))],
        compiler_params=params(),
    )(target, returned.reshape(owners * slots_each, rows, width))
    return (new_left[None, None], new_right[None, None], update)


def solution(mesh):
    placed = (
        P("dp", None, "shard", None),
        P(),
        P("dp", "shard", None, None, None),
        P("dp", "shard", None, None, None),
        P("dp", "shard", None, None, None),
        P("dp", "shard", None, None, None),
    )
    return jax.shard_map(
        shards,
        mesh=mesh,
        in_specs=placed,
        out_specs=(
            P("dp", "shard", None, None, None),
            P("dp", "shard", None, None, None),
            P("dp", "shard", None),
        ),
        check_vma=False,
    )
```

time: 104 us -> 104 us (level)
  matrix products: 6.22 us -> 0 us
  Pallas kernels: 7.48 us -> 12.4 us
  waiting for transfers between devices: 29 us -> 31.1 us
    dot_general x2 -> x0, matrix products: 6.22 us -> none  [the longest x1 3.93 us: shards(): jnp.einsum('cji,cjk->cik', blocks, blocks, preferred_element_type=jnp.flo...]
    pallas_call x3 -> x5, Pallas kernels: 3.85 us -> 8.8 us  [the longest x1 5.01 us: shards(): pl.pallas_call(factors, grid=(slots_each,), out_shape=[jax.ShapeDtypeStru...]
    ppermute x1, waiting for transfers between devices: 0.01 us -> 1.94 us  [shards(): from_left_high = lax.ppermute(near_right, 'dp', rightward)]
    all_to_all x1, waiting for transfers between devices: 21.7 us -> 23.5 us  [shards(): lax.all_to_all(finished, 'shard', split_axis=0, concat_axis=0, tiled=True)]
    ppermute x1, waiting for transfers between devices: 4.14 us -> 5.61 us  [shards(): from_left_low = lax.ppermute(to_right, 'dp', rightward)]
    ppermute x1, waiting for transfers between devices: 1.46 us -> 0.01 us  [shards(): from_right_low = lax.ppermute(near_left, 'dp', leftward)]
    ppermute x1, waiting for transfers between devices: 1.06 us -> 0.01 us  [shards(): from_right_high = lax.ppermute(to_left, 'dp', leftward)]
  transfers between devices with their start and end apart: 7 -> 7, of which waited for: 5 -> 3; matrix products, arithmetic and copies ran while one was open for 9% -> 2% of each run, Pallas kernels for 1% -> 6%
where the time goes in v3:
time: 104 us
  blocking collectives  42.1 us (40%)
  waiting for transfers between devices  31.1 us (30%)
  starting transfers between devices  15.2 us (15%)
  Pallas kernels  12.4 us (12%)
  local copies, waits for them, and re-layouts  1.09 us (1%)
    all_to_all x1, blocking collectives, shards(): lax.all_to_all(outgoing.reshape(owners, slots_each, rows, width), 'shard'...  42.1 us
    all_to_all x1, waiting for transfers between devices, shards(): lax.all_to_all(finished, 'shard', split_axis=0, concat_axis=0, tiled=True)  23.5 us
    all_to_all x1, starting transfers between devices, shards(): lax.all_to_all(finished, 'shard', split_axis=0, concat_axis=0, tiled=True)  6.19 us
    ppermute x1, waiting for transfers between devices, shards(): from_left_low = lax.ppermute(to_right, 'dp', rightward)  5.61 us
    pallas_call x1, Pallas kernels, shards(): pl.pallas_call(factors, grid=(slots_each,), out_shape=[jax.ShapeDtypeStru...  5.01 us
    pallas_call x1, Pallas kernels, shards(): pl.pallas_call(precondition, out_shape=jax.ShapeDtypeStruct((owners, slot...  2.77 us
    ppermute x1, starting transfers between devices, shards(): from_right_low = lax.ppermute(near_left, 'dp', leftward)  2.57 us
    pallas_call x2, Pallas kernels, staged(): pl.pallas_call(functools.partial(stage, replicas, wanted), out_shape=[pie...  2.28 us
  transfers between devices with their start and end apart: 7, of which 3 were waited for; matrix products, arithmetic and copies ran while one was open for 2% of the time, Pallas kernels for 6%

profile of v3, /device:TPU:1, one launch (start us, length us, event | category | flops | bytes accessed | tf_op | source)
XLA Modules:
  0.0 103.6 jit_solution(15325229513521242616)
XLA Ops:
  0.6 1.1 %shard_map.86 = (bf16[32,8,512]{2,1,0:T(8,128)(2,1)S(1)}, bf16[32,8,512]{2,1,0:T(8,128)(2,1)S(1)}) custom-call(bf16[256,8,512]{2,1,0:T(8,128)(2,1)} %bitcast.19), custom_call_target="tpu_custom_call" | custom-call | tf_op jit(solution)/shard_map/pallas_call | solution.py:136
  1.7 2.1 %collective-permute-start = (bf16[32,8,512]{2,1,0:T(8,128)(2,1)S(1)}, bf16[32,8,512]{2,1,0:T(8,128)(2,1)S(1)}, u32[]{:S(2)}, u32[]{:S(2)}) collective-permute-start(bf16[32,8,512]{2,1,0:T(8,128)(2,1)S(1)} %get-tuple-element.15), channel_id=1, source_target_pairs={{0,64},{64,128},{128,192},{192,0},{1,65},{65,129},{129,193},{193,1... | collective-permute-start | bytes 786440 | tf_op jit(solution)/shard_map/ppermute | solution.py:147
  3.8 1.4 %collective-permute-start.1 = (bf16[32,8,512]{2,1,0:T(8,128)(2,1)S(1)}, bf16[32,8,512]{2,1,0:T(8,128)(2,1)S(1)}, u32[]{:S(2)}, u32[]{:S(2)}) collective-permute-start(bf16[32,8,512]{2,1,0:T(8,128)(2,1)S(1)} %get-tuple-element.16), channel_id=1, source_target_pairs={{0,192},{64,0},{128,64},{192,128},{1,193},{65,1},{129,65},{193,129... | collective-permute-start | bytes 786440 | tf_op jit(solution)/shard_map/ppermute | solution.py:148
  5.2 1.2 %shard_map.85 = (bf16[32,8,512]{2,1,0:T(8,128)(2,1)S(1)}, bf16[32,8,512]{2,1,0:T(8,128)(2,1)S(1)}, bf16[32,8,512]{2,1,0:T(8,128)(2,1)S(1)}, bf16[32,8,512]{2,1,0:T(8,128)(2,1)S(1)}) custom-call(bf16[256,8,512]{2,1,0:T(8,128)(2,1)} %bitcast.20), custom_call_target="tpu_custom_call" | custom-call | tf_op jit(solution)/shard_map/pallas_call | solution.py:136
  6.4 0.2 collective-permute-start.3
  6.6 2.6 %collective-permute-start.4 = (bf16[32,8,512]{2,1,0:T(8,128)(2,1)S(1)}, bf16[32,8,512]{2,1,0:T(8,128)(2,1)S(1)}, u32[]{:S(2)}, u32[]{:S(2)}) collective-permute-start(bf16[32,8,512]{2,1,0:T(8,128)(2,1)S(1)} %get-tuple-element.19), channel_id=1, source_target_pairs={{0,192},{64,0},{128,64},{192,128},{1,193},{65,1},{129,65},{193,129... | collective-permute-start | bytes 786440 | tf_op jit(solution)/shard_map/ppermute | solution.py:150
  9.2 0.7 fusion.1
  9.9 1.1 %dynamic-slice_bitcast_fusion.own_ref = bf16[64,8,512]{2,1,0:T(8,128)(2,1)S(1)} fusion(bf16[1,256,8,512]{3,2,1,0:T(8,128)(2,1)} %param.6, s32[]{:T(128)S(6)} %select_n.4), kind=kLoop, calls=%fused_computation | loop fusion | bytes 1048580 | tf_op jit(solution)/shard_map/dynamic_slice | solution.py:160
  10.9 0.0 collective-permute-done.low_ref
  11.0 0.1 shard_map.87
  11.1 1.0 collective-permute-start.2
  12.1 1.8 %collective-permute-start.5 = (bf16[32,8,512]{2,1,0:T(8,128)(2,1)S(1)}, bf16[32,8,512]{2,1,0:T(8,128)(2,1)S(1)}, u32[]{:S(2)}, u32[]{:S(2)}) collective-permute-start(bf16[32,8,512]{2,1,0:T(8,128)(2,1)S(1)} %get-tuple-element.20), channel_id=1, source_target_pairs={{0,192},{64,0},{128,64},{192,128},{1,193},{65,1},{129,65},{193,129... | collective-permute-start | bytes 786440 | tf_op jit(solution)/shard_map/ppermute | solution.py:159
  13.9 0.2 convert_reduce_fusion
  14.1 0.0 copy-start
  14.1 0.0 copy-start.1
  14.1 1.9 %collective-permute-done.3.lh_ref = bf16[32,8,512]{2,1,0:T(8,128)(2,1)S(1)} collective-permute-done((bf16[32,8,512]{2,1,0:T(8,128)(2,1)S(1)}, bf16[32,8,512]{2,1,0:T(8,128)(2,1)S(1)}, u32[]{:S(2)}, u32[]{:S(2)}) %collective-permute-start.3) | collective-permute-done | bytes 262176 | tf_op jit(solution)/shard_map/ppermute | solution.py:149
  16.0 5.6 %collective-permute-done.2.ll_ref = bf16[32,8,512]{2,1,0:T(8,128)(2,1)S(1)} collective-permute-done((bf16[32,8,512]{2,1,0:T(8,128)(2,1)S(1)}, bf16[32,8,512]{2,1,0:T(8,128)(2,1)S(1)}, u32[]{:S(2)}, u32[]{:S(2)}) %collective-permute-start.2) | collective-permute-done | bytes 262176 | tf_op jit(solution)/shard_map/ppermute | solution.py:158
  21.6 0.9 shard_map.88
  22.5 42.1 %all_to_all.10.arrived_ref = bf16[64,2,8,512]{3,2,1,0:T(8,128)(2,1)S(1)} all-to-all(bf16[64,2,8,512]{3,2,1,0:T(8,128)(2,1)S(1)} %bitcast.16), channel_id=1, replica_groups=mesh['dp'=4,'shard'=64] {'shard'}, dimensions={0} | all-to-all | bytes 2097152 | tf_op jit(solution)/shard_map/all_to_all | solution.py:174
  64.7 2.8 %shard_map.90 = bf16[64,2,8,512]{3,2,1,0:T(8,128)(2,1)} custom-call(bf16[64,2,8,512]{3,2,1,0:T(8,128)(2,1)S(1)} %all_to_all.10.arrived_ref, bf16[2,512,512]{2,1,0:T(8,128)(2,1)S(1)} %bitcast.17, bf16[2,512,512]{2,1,0:T(8,128)(2,1)S(1)} %bitcast.18), custom_call_target="tpu_custom_call" | custom-call | tf_op jit(solution)/shard_map/pallas_call | solution.py:177
  67.4 6.2 %all-to-all-start.1 = ((bf16[64,2,8,512]{3,2,1,0:T(8,128)(2,1)}), bf16[64,2,8,512]{3,2,1,0:T(8,128)(2,1)S(1)}, u32[]{:S(2)}, u32[]{:S(2)}) async-start(bf16[64,2,8,512]{3,2,1,0:T(8,128)(2,1)} %shard_map.90), calls=%async_computation.1 | async-start | bytes 2097152 | tf_op jit(solution)/shard_map/all_to_all | solution.py:185
  73.6 5.0 %shard_map.89 = (f32[2,512,512]{2,1,0:T(8,128)}, f32[2,512,512]{2,1,0:T(8,128)}) custom-call(s32[1]{0:T(128)} %bitcast.1.count_ref, bf16[64,2,8,512]{3,2,1,0:T(8,128)(2,1)S(1)} %all_to_all.10.arrived_ref, f32[2,512,512]{2,1,0:T(8,128)} %bitcast.21, f32[2,512,512]{2,1,0:T(8,128)} %bitcast.22), custom_call_target="tpu_custom_call" | custom-call | flops 2147483648 | bytes 9437184 | tf_op jit(solution)/shard_map/pallas_call | solution.py:189
  78.6 23.5 %all-to-all-done.1 = bf16[64,2,8,512]{3,2,1,0:T(8,128)(2,1)S(1)} async-done(((bf16[64,2,8,512]{3,2,1,0:T(8,128)(2,1)}), bf16[64,2,8,512]{3,2,1,0:T(8,128)(2,1)S(1)}, u32[]{:S(2)}, u32[]{:S(2)}) %all-to-all-start.1) | async-done | bytes 1048608 | tf_op jit(solution)/shard_map/all_to_all | solution.py:185
  102.2 1.4 %shard_map.91 = bf16[64,8,512]{2,1,0:T(8,128)(2,1)} custom-call(s32[64]{0:T(128)S(1)} %multiply_add_fusion.target_ref, bf16[128,8,512]{2,1,0:T(8,128)(2,1)S(1)} %bitcast.15), custom_call_target="tpu_custom_call" | custom-call | tf_op jit(solution)/shard_map/pallas_call | solution.py:206
  (8 shorter events, 0.0 us)
Async XLA Ops:
  0.6 8.5 %copy-start.2 = (s32[256,1]{0,1:T(1,128)S(1)}, s32[256,1]{0,1:T(1,128)}, u32[]{:S(2)}) copy-start(s32[256,1]{0,1:T(1,128)} %param.7) | copy-start | bytes 3076
  1.7 9.2 %collective-permute-start = (bf16[32,8,512]{2,1,0:T(8,128)(2,1)S(1)}, bf16[32,8,512]{2,1,0:T(8,128)(2,1)S(1)}, u32[]{:S(2)}, u32[]{:S(2)}) collective-permute-start(bf16[32,8,512]{2,1,0:T(8,128)(2,1)S(1)} %get-tuple-element.15), channel_id=1, source_target_pairs={{0,64},{64,128},{128,192},{192,0},{1,65},{65,129},{129,193},{193,1... | collective-permute-start | bytes 786440 | tf_op jit(solution)/shard_map/ppermute | solution.py:147
  3.8 7.1 %collective-permute-start.1 = (bf16[32,8,512]{2,1,0:T(8,128)(2,1)S(1)}, bf16[32,8,512]{2,1,0:T(8,128)(2,1)S(1)}, u32[]{:S(2)}, u32[]{:S(2)}) collective-permute-start(bf16[32,8,512]{2,1,0:T(8,128)(2,1)S(1)} %get-tuple-element.16), channel_id=1, source_target_pairs={{0,192},{64,0},{128,64},{192,128},{1,193},{65,1},{129,65},{193,129... | collective-permute-start | bytes 786440 | tf_op jit(solution)/shard_map/ppermute | solution.py:148
  6.4 9.6 %collective-permute-start.3 = (bf16[32,8,512]{2,1,0:T(8,128)(2,1)S(1)}, bf16[32,8,512]{2,1,0:T(8,128)(2,1)S(1)}, u32[]{:S(2)}, u32[]{:S(2)}) collective-permute-start(bf16[32,8,512]{2,1,0:T(8,128)(2,1)S(1)} %get-tuple-element.18), channel_id=1, source_target_pairs={{0,64},{64,128},{128,192},{192,0},{1,65},{65,129},{129,193},{193,1... | collective-permute-start | bytes 786440 | tf_op jit(solution)/shard_map/ppermute | solution.py:149
  6.6 9.4 %collective-permute-start.4 = (bf16[32,8,512]{2,1,0:T(8,128)(2,1)S(1)}, bf16[32,8,512]{2,1,0:T(8,128)(2,1)S(1)}, u32[]{:S(2)}, u32[]{:S(2)}) collective-permute-start(bf16[32,8,512]{2,1,0:T(8,128)(2,1)S(1)} %get-tuple-element.19), channel_id=1, source_target_pairs={{0,192},{64,0},{128,64},{192,128},{1,193},{65,1},{129,65},{193,129... | collective-permute-start | bytes 786440 | tf_op jit(solution)/shard_map/ppermute | solution.py:150
  11.1 10.5 %collective-permute-start.2 = (bf16[32,8,512]{2,1,0:T(8,128)(2,1)S(1)}, bf16[32,8,512]{2,1,0:T(8,128)(2,1)S(1)}, u32[]{:S(2)}, u32[]{:S(2)}) collective-permute-start(bf16[32,8,512]{2,1,0:T(8,128)(2,1)S(1)} %get-tuple-element.17), channel_id=1, source_target_pairs={{0,64},{64,128},{128,192},{192,0},{1,65},{65,129},{129,193},{193,1... | collective-permute-start | bytes 786440 | tf_op jit(solution)/shard_map/ppermute | solution.py:158
  12.1 9.5 %collective-permute-start.5 = (bf16[32,8,512]{2,1,0:T(8,128)(2,1)S(1)}, bf16[32,8,512]{2,1,0:T(8,128)(2,1)S(1)}, u32[]{:S(2)}, u32[]{:S(2)}) collective-permute-start(bf16[32,8,512]{2,1,0:T(8,128)(2,1)S(1)} %get-tuple-element.20), channel_id=1, source_target_pairs={{0,192},{64,0},{128,64},{192,128},{1,193},{65,1},{129,65},{193,129... | collective-permute-start | bytes 786440 | tf_op jit(solution)/shard_map/ppermute | solution.py:159
  14.1 50.6 %copy-start = (bf16[1,1,2,512,512]{4,3,2,1,0:T(8,128)(2,1)S(1)}, bf16[1,1,2,512,512]{4,3,2,1,0:T(8,128)(2,1)}, u32[]{:S(2)}) copy-start(bf16[1,1,2,512,512]{4,3,2,1,0:T(8,128)(2,1)} %param.10) | copy-start | bytes 3145732
  14.1 50.6 %copy-start.1 = (bf16[1,1,2,512,512]{4,3,2,1,0:T(8,128)(2,1)S(1)}, bf16[1,1,2,512,512]{4,3,2,1,0:T(8,128)(2,1)}, u32[]{:S(2)}) copy-start(bf16[1,1,2,512,512]{4,3,2,1,0:T(8,128)(2,1)} %param.11) | copy-start | bytes 3145732
  67.4 34.8 %all-to-all-start.1 = ((bf16[64,2,8,512]{3,2,1,0:T(8,128)(2,1)}), bf16[64,2,8,512]{3,2,1,0:T(8,128)(2,1)S(1)}, u32[]{:S(2)}, u32[]{:S(2)}) async-start(bf16[64,2,8,512]{3,2,1,0:T(8,128)(2,1)} %shard_map.90), calls=%async_computation.1 | async-start | bytes 2097152 | tf_op jit(solution)/shard_map/all_to_all | solution.py:185

commit v4 on v3

--- a/solution.py
+++ b/solution.py
@@ -41,6 +41,26 @@
     lax.fori_loop(0, half, one, 0, unroll=8)
 
 
+def slots_of(owners, slots, owner_ref, target_ref, count_ref, seen):
+    group = target_ref.shape[0]
+    first = lax.axis_index("dp") * group
+
+    def clear(o, _):
+        seen[o] = 0
+        return 0
+
+    def one(b, _):
+        o = owner_ref[first + b]
+        c = seen[o]
+        target_ref[b] = o * slots + c
+        seen[o] = c + 1
+        return 0
+
+    lax.fori_loop(0, owners, clear, 0, unroll=8)
+    lax.fori_loop(0, group, one, 0, unroll=4)
+    count_ref[0] = seen[lax.axis_index("shard")]
+
+
 def mean_and_route(replicas, target_ref, own_ref, ll_ref, lh_ref, rl_ref, rh_ref, out_ref):
     half = ll_ref.shape[0]
     out_ref[...] = jnp.zeros_like(out_ref)
@@ -55,9 +75,10 @@
     lax.fori_loop(0, half, one, 0, unroll=4)
 
 
-def precondition(arrived_ref, lroot_ref, rroot_ref, out_ref, block):
+def precondition(arrived_ref, lroot_ref, rroot_ref, out_ref, block, finished, sems):
     senders, slots, rows, width = arrived_ref.shape
     entries = senders * rows * width
+    powers, pres, copies = [], [], []
     for c in range(slots):
         power = jnp.zeros((rows, width), jnp.float32)
         for s in range(0, senders, 2):
@@ -65,13 +86,23 @@
             second = arrived_ref[s + 1, c].astype(jnp.float32)
             power = power + (first * first + second * second)
             block[c, pl.ds(s * rows, 2 * rows), :] = jnp.concatenate([first, second], axis=0).astype(jnp.bfloat16)
+        powers.append(jnp.sum(power, keepdims=True))
+    for c in range(slots):
         half = jnp.dot(lroot_ref[c], block[c], preferred_element_type=jnp.float32).astype(jnp.bfloat16)
-        pre = jnp.dot(half, rroot_ref[c], preferred_element_type=jnp.float32)
-        grad_power = jnp.sum(power, keepdims=True)
+        pres.append(jnp.dot(half, rroot_ref[c], preferred_element_type=jnp.float32))
+    each = senders // sems.shape[1]
+    for c in range(slots):
+        pre = pres[c]
         pre_power = jnp.sum(pre * pre, keepdims=True)
-        ratio = jnp.sqrt(grad_power / entries + EPS) / jnp.sqrt(pre_power / entries + EPS)
-        for s in range(senders):
-            out_ref[s, c] = (pre[s * rows : (s + 1) * rows] * ratio).astype(jnp.bfloat16)
+        ratio = jnp.sqrt(powers[c] / entries + EPS) / jnp.sqrt(pre_power / entries + EPS)
+        for k in range(sems.shape[1]):
+            for s in range(k * each, (k + 1) * each):
+                finished[c, s] = (pre[s * rows : (s + 1) * rows] * ratio).astype(jnp.bfloat16)
+            span = pl.ds(k * each, each)
+            copies.append(pltpu.make_async_copy(finished.at[c, span], out_ref.at[span, c], sems.at[c, k]))
+            copies[-1].start()
+    for copy in copies:
+        copy.wait()
 
 
 def factors(count_ref, arrived_ref, left_ref, right_ref, new_left_ref, new_right_ref, block):
@@ -155,14 +186,18 @@
         out_specs=[in_vmem()] * 2,
         compiler_params=params(),
     )(own_low, own_high, low, high)
+    late_grads, late_owner, to_right = lax.optimization_barrier((grads, owner, to_right))
     from_left_low = lax.ppermute(to_right, "dp", rightward)
     from_right_high = lax.ppermute(to_left, "dp", leftward)
-    own = lax.dynamic_slice_in_dim(grads[0], me * group, group)
-    table = lax.dynamic_slice_in_dim(owner[:, 0], lax.axis_index("dp") * group, group)
-    index = jnp.arange(group, dtype=jnp.int32)
-    same = (table[:, None] == table[None, :]) & (index[None, :] < index[:, None])
-    slots = jnp.sum(same.astype(jnp.int32), axis=1)
-    target = table * slots_each + slots
+    own = lax.dynamic_slice_in_dim(late_grads[0], me * group, group)
+    target, count = pl.pallas_call(
+        functools.partial(slots_of, owners, slots_each),
+        out_shape=[pltpu.SMEM((group,), jnp.int32), pltpu.SMEM((1,), jnp.int32)],
+        in_specs=[in_smem()],
+        out_specs=[in_smem()] * 2,
+        scratch_shapes=[pltpu.SMEM((owners,), jnp.int32)],
+        compiler_params=params(),
+    )(late_owner[:, 0])
     target = pltpu.with_memory_space_constraint(target, pltpu.SMEM)
     outgoing = pl.pallas_call(
         functools.partial(mean_and_route, replicas),
@@ -176,14 +211,17 @@
     )
     finished = pl.pallas_call(
         precondition,
-        out_shape=jax.ShapeDtypeStruct((owners, slots_each, rows, width), jnp.bfloat16),
+        out_shape=pltpu.HBM((owners, slots_each, rows, width), jnp.bfloat16),
         in_specs=[in_vmem()] * 3,
-        out_specs=in_vmem(),
-        scratch_shapes=[pltpu.VMEM((slots_each, owners * rows, width), jnp.bfloat16)],
+        out_specs=in_hbm(),
+        scratch_shapes=[
+            pltpu.VMEM((slots_each, owners * rows, width), jnp.bfloat16),
+            pltpu.VMEM((slots_each, owners, rows, width), jnp.bfloat16),
+            pltpu.SemaphoreType.DMA((slots_each, 2)),
+        ],
         compiler_params=params(),
     )(arrived, left_root[0, 0], right_root[0, 0])
     returned = lax.all_to_all(finished, "shard", split_axis=0, concat_axis=0, tiled=True)
-    count = jnp.sum((table == lax.axis_index("shard")).astype(jnp.int32)).reshape(1)
     order = left_factor.shape[3:]
     of_slot = pl.BlockSpec((1, *order), lambda c: (c, 0, 0))
     new_left, new_right = pl.pallas_call(

time: 104 us -> 103 us (level)
    ppermute x1, waiting for transfers between devices: 1.94 us -> 0.7 us  [shards(): from_left_high = lax.ppermute(near_right, 'dp', rightward)]
    ppermute x1, waiting for transfers between devices: 0.01 us -> 1.16 us  [shards(): high = lax.ppermute(far_high, 'dp', leftward)]
    pallas_call x1 -> x2, Pallas kernels: 2.77 us -> 3.66 us  [the longest x1 2.66 us: shards(): pl.pallas_call(precondition, out_shape=pltpu.HBM((owners, slots_each, row...]
  transfers between devices with their start and end apart: 7 -> 7, of which waited for: 3 -> 4; matrix products, arithmetic and copies ran while one was open for 2% -> 1% of each run, Pallas kernels for 6% -> 7%
where the time goes in v4:
time: 103 us
  blocking collectives  42.3 us (41%)
  waiting for transfers between devices  31.7 us (31%)
  starting transfers between devices  15.2 us (15%)
  Pallas kernels  11.6 us (11%)
  local copies, waits for them, and re-layouts  1.1 us (1%)
    all_to_all x1, blocking collectives, shards(): lax.all_to_all(outgoing.reshape(owners, slots_each, rows, width), 'shard'...  42.3 us
    all_to_all x1, waiting for transfers between devices, shards(): lax.all_to_all(finished, 'shard', split_axis=0, concat_axis=0, tiled=True)  24.2 us
    all_to_all x1, starting transfers between devices, shards(): lax.all_to_all(finished, 'shard', split_axis=0, concat_axis=0, tiled=True)  6.21 us
    ppermute x1, waiting for transfers between devices, shards(): from_left_low = lax.ppermute(to_right, 'dp', rightward)  5.61 us
    pallas_call x1, Pallas kernels, shards(): pl.pallas_call(factors, grid=(slots_each,), out_shape=[jax.ShapeDtypeStru...  4.37 us
    pallas_call x1, Pallas kernels, shards(): pl.pallas_call(precondition, out_shape=pltpu.HBM((owners, slots_each, row...  2.66 us
    ppermute x1, starting transfers between devices, shards(): from_right_low = lax.ppermute(near_left, 'dp', leftward)  2.57 us
    pallas_call x2, Pallas kernels, staged(): pl.pallas_call(functools.partial(stage, replicas, wanted), out_shape=[pie...  2.28 us
  transfers between devices with their start and end apart: 7, of which 4 were waited for; matrix products, arithmetic and copies ran while one was open for 1% of the time, Pallas kernels for 7%

profile of v4, /device:TPU:1, one launch (start us, length us, event | category | flops | bytes accessed | tf_op | source)
XLA Modules:
  0.0 102.5 jit_solution(11443829447651470605)
XLA Ops:
  0.6 1.1 %shard_map.86 = (bf16[32,8,512]{2,1,0:T(8,128)(2,1)S(1)}, bf16[32,8,512]{2,1,0:T(8,128)(2,1)S(1)}) custom-call(bf16[256,8,512]{2,1,0:T(8,128)(2,1)} %bitcast.17), custom_call_target="tpu_custom_call" | custom-call | tf_op jit(solution)/shard_map/pallas_call | solution.py:167
  1.7 0.0 copy-start.2
  1.7 2.1 %collective-permute-start = (bf16[32,8,512]{2,1,0:T(8,128)(2,1)S(1)}, bf16[32,8,512]{2,1,0:T(8,128)(2,1)S(1)}, u32[]{:S(2)}, u32[]{:S(2)}) collective-permute-start(bf16[32,8,512]{2,1,0:T(8,128)(2,1)S(1)} %get-tuple-element.20), channel_id=1, source_target_pairs={{0,64},{64,128},{128,192},{192,0},{1,65},{65,129},{129,193},{193,1... | collective-permute-start | bytes 786440 | tf_op jit(solution)/shard_map/ppermute | solution.py:178
  3.8 1.4 %collective-permute-start.1 = (bf16[32,8,512]{2,1,0:T(8,128)(2,1)S(1)}, bf16[32,8,512]{2,1,0:T(8,128)(2,1)S(1)}, u32[]{:S(2)}, u32[]{:S(2)}) collective-permute-start(bf16[32,8,512]{2,1,0:T(8,128)(2,1)S(1)} %get-tuple-element.21), channel_id=1, source_target_pairs={{0,192},{64,0},{128,64},{192,128},{1,193},{65,1},{129,65},{193,129... | collective-permute-start | bytes 786440 | tf_op jit(solution)/shard_map/ppermute | solution.py:179
  5.2 1.2 %shard_map.85 = (bf16[32,8,512]{2,1,0:T(8,128)(2,1)S(1)}, bf16[32,8,512]{2,1,0:T(8,128)(2,1)S(1)}, bf16[32,8,512]{2,1,0:T(8,128)(2,1)S(1)}, bf16[32,8,512]{2,1,0:T(8,128)(2,1)S(1)}) custom-call(bf16[256,8,512]{2,1,0:T(8,128)(2,1)} %bitcast.18), custom_call_target="tpu_custom_call" | custom-call | tf_op jit(solution)/shard_map/pallas_call | solution.py:167
  6.4 0.2 collective-permute-start.3
  6.6 2.6 %collective-permute-start.4 = (bf16[32,8,512]{2,1,0:T(8,128)(2,1)S(1)}, bf16[32,8,512]{2,1,0:T(8,128)(2,1)S(1)}, u32[]{:S(2)}, u32[]{:S(2)}) collective-permute-start(bf16[32,8,512]{2,1,0:T(8,128)(2,1)S(1)} %get-tuple-element.29), channel_id=1, source_target_pairs={{0,192},{64,0},{128,64},{192,128},{1,193},{65,1},{129,65},{193,129... | collective-permute-start | bytes 786440 | tf_op jit(solution)/shard_map/ppermute | solution.py:181
  9.2 0.0 collective-permute-done.low_ref
  9.2 1.2 %collective-permute-done.1.high_ref = bf16[32,8,512]{2,1,0:T(8,128)(2,1)S(1)} collective-permute-done((bf16[32,8,512]{2,1,0:T(8,128)(2,1)S(1)}, bf16[32,8,512]{2,1,0:T(8,128)(2,1)S(1)}, u32[]{:S(2)}, u32[]{:S(2)}) %collective-permute-start.1) | collective-permute-done | bytes 262176 | tf_op jit(solution)/shard_map/ppermute | solution.py:179
  10.3 0.1 shard_map.87
  10.5 1.6 %collective-permute-start.2 = (bf16[32,8,512]{2,1,0:T(8,128)(2,1)S(1)}, bf16[32,8,512]{2,1,0:T(8,128)(2,1)S(1)}, u32[]{:S(2)}, u32[]{:S(2)}) collective-permute-start(bf16[32,8,512]{2,1,0:T(8,128)(2,1)S(1)} %get-tuple-element.27), channel_id=1, source_target_pairs={{0,64},{64,128},{128,192},{192,0},{1,65},{65,129},{129,193},{193,1... | collective-permute-start | bytes 786440 | tf_op jit(solution)/shard_map/ppermute | solution.py:190
  12.1 1.1 %collective-permute-start.5 = (bf16[32,8,512]{2,1,0:T(8,128)(2,1)S(1)}, bf16[32,8,512]{2,1,0:T(8,128)(2,1)S(1)}, u32[]{:S(2)}, u32[]{:S(2)}) collective-permute-start(bf16[32,8,512]{2,1,0:T(8,128)(2,1)S(1)} %get-tuple-element.30), channel_id=1, source_target_pairs={{0,192},{64,0},{128,64},{192,128},{1,193},{65,1},{129,65},{193,129... | collective-permute-start | bytes 786440 | tf_op jit(solution)/shard_map/ppermute | solution.py:191
  13.2 1.0 shard_map.88
  14.2 1.1 %dynamic-slice_bitcast_fusion.own_ref = bf16[64,8,512]{2,1,0:T(8,128)(2,1)S(1)} fusion(bf16[1,256,8,512]{3,2,1,0:T(8,128)(2,1)} %param.6, s32[]{:T(128)S(6)} %select_n.3), kind=kLoop, calls=%fused_computation | loop fusion | bytes 1048580 | tf_op jit(solution)/shard_map/dynamic_slice | solution.py:192
  15.3 0.7 collective-permute-done.3.lh_ref
  16.0 0.0 collective-permute-done.4.rl_ref
  16.0 5.6 %collective-permute-done.2.ll_ref = bf16[32,8,512]{2,1,0:T(8,128)(2,1)S(1)} collective-permute-done((bf16[32,8,512]{2,1,0:T(8,128)(2,1)S(1)}, bf16[32,8,512]{2,1,0:T(8,128)(2,1)S(1)}, u32[]{:S(2)}, u32[]{:S(2)}) %collective-permute-start.2) | collective-permute-done | bytes 262176 | tf_op jit(solution)/shard_map/ppermute | solution.py:190
  21.6 0.3 shard_map.89
  22.0 42.3 %all_to_all.10.arrived_ref = bf16[64,2,8,512]{3,2,1,0:T(8,128)(2,1)S(1)} all-to-all(bf16[64,2,8,512]{3,2,1,0:T(8,128)(2,1)S(1)} %bitcast.13), channel_id=1, replica_groups=mesh['dp'=4,'shard'=64] {'shard'}, dimensions={0} | all-to-all | bytes 2097152 | tf_op jit(solution)/shard_map/all_to_all | solution.py:209
  64.3 2.7 %shard_map.91 = bf16[64,2,8,512]{3,2,1,0:T(8,128)(2,1)} custom-call(bf16[64,2,8,512]{3,2,1,0:T(8,128)(2,1)S(1)} %all_to_all.10.arrived_ref, bf16[2,512,512]{2,1,0:T(8,128)(2,1)S(1)} %bitcast.14, bf16[2,512,512]{2,1,0:T(8,128)(2,1)S(1)} %bitcast.15), custom_call_target="tpu_custom_call" | custom-call | tf_op jit(solution)/shard_map/pallas_call | solution.py:212
  66.9 6.2 %all-to-all-start.1 = ((bf16[64,2,8,512]{3,2,1,0:T(8,128)(2,1)}), bf16[64,2,8,512]{3,2,1,0:T(8,128)(2,1)S(1)}, u32[]{:S(2)}, u32[]{:S(2)}) async-start(bf16[64,2,8,512]{3,2,1,0:T(8,128)(2,1)} %shard_map.91), calls=%async_computation.1 | async-start | bytes 2097152 | tf_op jit(solution)/shard_map/all_to_all | solution.py:224
  73.2 4.4 %shard_map.90 = (f32[2,512,512]{2,1,0:T(8,128)}, f32[2,512,512]{2,1,0:T(8,128)}) custom-call(s32[1]{0:T(128)S(4)} %get-tuple-element.24.count_ref, bf16[64,2,8,512]{3,2,1,0:T(8,128)(2,1)S(1)} %all_to_all.10.arrived_ref, f32[2,512,512]{2,1,0:T(8,128)} %bitcast.19, f32[2,512,512]{2,1,0:T(8,128)} %bitcast.20), custom_call_target="tpu_custom_call" | custom-call | flops 2147483648 | bytes 9437184 | tf_op jit(solution)/shard_map/pallas_call | solution.py:227
  77.5 24.2 %all-to-all-done.1 = bf16[64,2,8,512]{3,2,1,0:T(8,128)(2,1)S(1)} async-done(((bf16[64,2,8,512]{3,2,1,0:T(8,128)(2,1)}), bf16[64,2,8,512]{3,2,1,0:T(8,128)(2,1)S(1)}, u32[]{:S(2)}, u32[]{:S(2)}) %all-to-all-start.1) | async-done | bytes 1048608 | tf_op jit(solution)/shard_map/all_to_all | solution.py:224
  101.7 0.8 shard_map.92
  (6 shorter events, 0.0 us)
Async XLA Ops:
  1.7 11.5 %copy-start.2 = (s32[256,1]{0,1:T(1,128)S(1)}, s32[256,1]{0,1:T(1,128)}, u32[]{:S(2)}) copy-start(s32[256,1]{0,1:T(1,128)} %param.7) | copy-start | bytes 3076
  1.7 7.5 %collective-permute-start = (bf16[32,8,512]{2,1,0:T(8,128)(2,1)S(1)}, bf16[32,8,512]{2,1,0:T(8,128)(2,1)S(1)}, u32[]{:S(2)}, u32[]{:S(2)}) collective-permute-start(bf16[32,8,512]{2,1,0:T(8,128)(2,1)S(1)} %get-tuple-element.20), channel_id=1, source_target_pairs={{0,64},{64,128},{128,192},{192,0},{1,65},{65,129},{129,193},{193,1... | collective-permute-start | bytes 786440 | tf_op jit(solution)/shard_map/ppermute | solution.py:178
  3.8 6.5 %collective-permute-start.1 = (bf16[32,8,512]{2,1,0:T(8,128)(2,1)S(1)}, bf16[32,8,512]{2,1,0:T(8,128)(2,1)S(1)}, u32[]{:S(2)}, u32[]{:S(2)}) collective-permute-start(bf16[32,8,512]{2,1,0:T(8,128)(2,1)S(1)} %get-tuple-element.21), channel_id=1, source_target_pairs={{0,192},{64,0},{128,64},{192,128},{1,193},{65,1},{129,65},{193,129... | collective-permute-start | bytes 786440 | tf_op jit(solution)/shard_map/ppermute | solution.py:179
  6.4 9.6 %collective-permute-start.3 = (bf16[32,8,512]{2,1,0:T(8,128)(2,1)S(1)}, bf16[32,8,512]{2,1,0:T(8,128)(2,1)S(1)}, u32[]{:S(2)}, u32[]{:S(2)}) collective-permute-start(bf16[32,8,512]{2,1,0:T(8,128)(2,1)S(1)} %get-tuple-element.28), channel_id=1, source_target_pairs={{0,64},{64,128},{128,192},{192,0},{1,65},{65,129},{129,193},{193,1... | collective-permute-start | bytes 786440 | tf_op jit(solution)/shard_map/ppermute | solution.py:180
  6.6 9.4 %collective-permute-start.4 = (bf16[32,8,512]{2,1,0:T(8,128)(2,1)S(1)}, bf16[32,8,512]{2,1,0:T(8,128)(2,1)S(1)}, u32[]{:S(2)}, u32[]{:S(2)}) collective-permute-start(bf16[32,8,512]{2,1,0:T(8,128)(2,1)S(1)} %get-tuple-element.29), channel_id=1, source_target_pairs={{0,192},{64,0},{128,64},{192,128},{1,193},{65,1},{129,65},{193,129... | collective-permute-start | bytes 786440 | tf_op jit(solution)/shard_map/ppermute | solution.py:181
  10.5 11.2 %collective-permute-start.2 = (bf16[32,8,512]{2,1,0:T(8,128)(2,1)S(1)}, bf16[32,8,512]{2,1,0:T(8,128)(2,1)S(1)}, u32[]{:S(2)}, u32[]{:S(2)}) collective-permute-start(bf16[32,8,512]{2,1,0:T(8,128)(2,1)S(1)} %get-tuple-element.27), channel_id=1, source_target_pairs={{0,64},{64,128},{128,192},{192,0},{1,65},{65,129},{129,193},{193,1... | collective-permute-start | bytes 786440 | tf_op jit(solution)/shard_map/ppermute | solution.py:190
  12.1 9.5 %collective-permute-start.5 = (bf16[32,8,512]{2,1,0:T(8,128)(2,1)S(1)}, bf16[32,8,512]{2,1,0:T(8,128)(2,1)S(1)}, u32[]{:S(2)}, u32[]{:S(2)}) collective-permute-start(bf16[32,8,512]{2,1,0:T(8,128)(2,1)S(1)} %get-tuple-element.30), channel_id=1, source_target_pairs={{0,192},{64,0},{128,64},{192,128},{1,193},{65,1},{129,65},{193,129... | collective-permute-start | bytes 786440 | tf_op jit(solution)/shard_map/ppermute | solution.py:191
  21.6 42.6 %copy-start = (bf16[1,1,2,512,512]{4,3,2,1,0:T(8,128)(2,1)S(1)}, bf16[1,1,2,512,512]{4,3,2,1,0:T(8,128)(2,1)}, u32[]{:S(2)}) copy-start(bf16[1,1,2,512,512]{4,3,2,1,0:T(8,128)(2,1)} %param.10) | copy-start | bytes 3145732
  21.6 42.6 %copy-start.1 = (bf16[1,1,2,512,512]{4,3,2,1,0:T(8,128)(2,1)S(1)}, bf16[1,1,2,512,512]{4,3,2,1,0:T(8,128)(2,1)}, u32[]{:S(2)}) copy-start(bf16[1,1,2,512,512]{4,3,2,1,0:T(8,128)(2,1)} %param.11) | copy-start | bytes 3145732
  66.9 34.8 %all-to-all-start.1 = ((bf16[64,2,8,512]{3,2,1,0:T(8,128)(2,1)}), bf16[64,2,8,512]{3,2,1,0:T(8,128)(2,1)S(1)}, u32[]{:S(2)}, u32[]{:S(2)}) async-start(bf16[64,2,8,512]{3,2,1,0:T(8,128)(2,1)} %shard_map.91), calls=%async_computation.1 | async-start | bytes 2097152 | tf_op jit(solution)/shard_map/all_to_all | solution.py:224

commit v5 on v4

--- a/solution.py
+++ b/solution.py
@@ -62,17 +62,12 @@
 
 
 def mean_and_route(replicas, target_ref, own_ref, ll_ref, lh_ref, rl_ref, rh_ref, out_ref):
+    out_ref[...] = jnp.zeros_like(out_ref)
     half = ll_ref.shape[0]
-    out_ref[...] = jnp.zeros_like(out_ref)
-
-    def one(b, _):
-        low = own_ref[b].astype(jnp.float32) + ll_ref[b].astype(jnp.float32) + rl_ref[b].astype(jnp.float32)
-        out_ref[target_ref[b]] = (low / replicas).astype(jnp.bfloat16)
-        high = own_ref[b + half].astype(jnp.float32) + lh_ref[b].astype(jnp.float32) + rh_ref[b].astype(jnp.float32)
-        out_ref[target_ref[b + half]] = (high / replicas).astype(jnp.bfloat16)
-        return 0
-
-    lax.fori_loop(0, half, one, 0, unroll=4)
+    for b in range(own_ref.shape[0]):
+        left, right, at = (ll_ref, rl_ref, b) if b < half else (lh_ref, rh_ref, b - half)
+        total = own_ref[b].astype(jnp.float32) + left[at].astype(jnp.float32) + right[at].astype(jnp.float32)
+        out_ref[target_ref[b]] = (total / replicas).astype(jnp.bfloat16)
 
 
 def precondition(arrived_ref, lroot_ref, rroot_ref, out_ref, block, finished, sems):

time: 103 us -> 103 us (level)
  no operation moved by 1% of the time
where the time goes in v5:
time: 103 us; the launch traced here: 102 us
  blocking collectives  42.3 us (41%)
  waiting for transfers between devices  31.7 us (31%)
  starting transfers between devices  15.2 us (15%)
  Pallas kernels  11.6 us (11%)
  local copies, waits for them, and re-layouts  1.1 us (1%)
    all_to_all x1, blocking collectives, shards(): lax.all_to_all(outgoing.reshape(owners, slots_each, rows, width), 'shard'...  42.3 us
    all_to_all x1, waiting for transfers between devices, shards(): lax.all_to_all(finished, 'shard', split_axis=0, concat_axis=0, tiled=True)  24.2 us
    all_to_all x1, starting transfers between devices, shards(): lax.all_to_all(finished, 'shard', split_axis=0, concat_axis=0, tiled=True)  6.2 us
    ppermute x1, waiting for transfers between devices, shards(): from_left_low = lax.ppermute(to_right, 'dp', rightward)  5.61 us
    pallas_call x1, Pallas kernels, shards(): pl.pallas_call(factors, grid=(slots_each,), out_shape=[jax.ShapeDtypeStru...  4.37 us
    pallas_call x1, Pallas kernels, shards(): pl.pallas_call(precondition, out_shape=pltpu.HBM((owners, slots_each, row...  2.66 us
    ppermute x1, starting transfers between devices, shards(): from_right_low = lax.ppermute(near_left, 'dp', leftward)  2.57 us
    pallas_call x2, Pallas kernels, staged(): pl.pallas_call(functools.partial(stage, replicas, wanted), out_shape=[pie...  2.28 us
  transfers between devices with their start and end apart: 7, of which 4 were waited for; matrix products, arithmetic and copies ran while one was open for 1% of the time, Pallas kernels for 7%

profile of v5, /device:TPU:1, one launch (start us, length us, event | category | flops | bytes accessed | tf_op | source)
XLA Modules:
  0.0 102.5 jit_solution(12021891883751782618)
XLA Ops:
  0.6 1.1 %shard_map.86 = (bf16[32,8,512]{2,1,0:T(8,128)(2,1)S(1)}, bf16[32,8,512]{2,1,0:T(8,128)(2,1)S(1)}) custom-call(bf16[256,8,512]{2,1,0:T(8,128)(2,1)} %bitcast.17), custom_call_target="tpu_custom_call" | custom-call | tf_op jit(solution)/shard_map/pallas_call | solution.py:162
  1.7 0.0 copy-start.2
  1.7 2.1 %collective-permute-start = (bf16[32,8,512]{2,1,0:T(8,128)(2,1)S(1)}, bf16[32,8,512]{2,1,0:T(8,128)(2,1)S(1)}, u32[]{:S(2)}, u32[]{:S(2)}) collective-permute-start(bf16[32,8,512]{2,1,0:T(8,128)(2,1)S(1)} %get-tuple-element.20), channel_id=1, source_target_pairs={{0,64},{64,128},{128,192},{192,0},{1,65},{65,129},{129,193},{193,1... | collective-permute-start | bytes 786440 | tf_op jit(solution)/shard_map/ppermute | solution.py:173
  3.8 1.4 %collective-permute-start.1 = (bf16[32,8,512]{2,1,0:T(8,128)(2,1)S(1)}, bf16[32,8,512]{2,1,0:T(8,128)(2,1)S(1)}, u32[]{:S(2)}, u32[]{:S(2)}) collective-permute-start(bf16[32,8,512]{2,1,0:T(8,128)(2,1)S(1)} %get-tuple-element.21), channel_id=1, source_target_pairs={{0,192},{64,0},{128,64},{192,128},{1,193},{65,1},{129,65},{193,129... | collective-permute-start | bytes 786440 | tf_op jit(solution)/shard_map/ppermute | solution.py:174
  5.2 1.2 %shard_map.85 = (bf16[32,8,512]{2,1,0:T(8,128)(2,1)S(1)}, bf16[32,8,512]{2,1,0:T(8,128)(2,1)S(1)}, bf16[32,8,512]{2,1,0:T(8,128)(2,1)S(1)}, bf16[32,8,512]{2,1,0:T(8,128)(2,1)S(1)}) custom-call(bf16[256,8,512]{2,1,0:T(8,128)(2,1)} %bitcast.18), custom_call_target="tpu_custom_call" | custom-call | tf_op jit(solution)/shard_map/pallas_call | solution.py:162
  6.4 0.2 collective-permute-start.3
  6.6 2.6 %collective-permute-start.4 = (bf16[32,8,512]{2,1,0:T(8,128)(2,1)S(1)}, bf16[32,8,512]{2,1,0:T(8,128)(2,1)S(1)}, u32[]{:S(2)}, u32[]{:S(2)}) collective-permute-start(bf16[32,8,512]{2,1,0:T(8,128)(2,1)S(1)} %get-tuple-element.29), channel_id=1, source_target_pairs={{0,192},{64,0},{128,64},{192,128},{1,193},{65,1},{129,65},{193,129... | collective-permute-start | bytes 786440 | tf_op jit(solution)/shard_map/ppermute | solution.py:176
  9.2 0.0 collective-permute-done.low_ref
  9.2 1.2 %collective-permute-done.1.high_ref = bf16[32,8,512]{2,1,0:T(8,128)(2,1)S(1)} collective-permute-done((bf16[32,8,512]{2,1,0:T(8,128)(2,1)S(1)}, bf16[32,8,512]{2,1,0:T(8,128)(2,1)S(1)}, u32[]{:S(2)}, u32[]{:S(2)}) %collective-permute-start.1) | collective-permute-done | bytes 262176 | tf_op jit(solution)/shard_map/ppermute | solution.py:174
  10.3 0.1 shard_map.87
  10.5 1.6 %collective-permute-start.2 = (bf16[32,8,512]{2,1,0:T(8,128)(2,1)S(1)}, bf16[32,8,512]{2,1,0:T(8,128)(2,1)S(1)}, u32[]{:S(2)}, u32[]{:S(2)}) collective-permute-start(bf16[32,8,512]{2,1,0:T(8,128)(2,1)S(1)} %get-tuple-element.27), channel_id=1, source_target_pairs={{0,64},{64,128},{128,192},{192,0},{1,65},{65,129},{129,193},{193,1... | collective-permute-start | bytes 786440 | tf_op jit(solution)/shard_map/ppermute | solution.py:185
  12.1 1.1 %collective-permute-start.5 = (bf16[32,8,512]{2,1,0:T(8,128)(2,1)S(1)}, bf16[32,8,512]{2,1,0:T(8,128)(2,1)S(1)}, u32[]{:S(2)}, u32[]{:S(2)}) collective-permute-start(bf16[32,8,512]{2,1,0:T(8,128)(2,1)S(1)} %get-tuple-element.30), channel_id=1, source_target_pairs={{0,192},{64,0},{128,64},{192,128},{1,193},{65,1},{129,65},{193,129... | collective-permute-start | bytes 786440 | tf_op jit(solution)/shard_map/ppermute | solution.py:186
  13.2 1.0 shard_map.88
  14.2 1.1 %dynamic-slice_bitcast_fusion.own_ref = bf16[64,8,512]{2,1,0:T(8,128)(2,1)S(1)} fusion(bf16[1,256,8,512]{3,2,1,0:T(8,128)(2,1)} %param.6, s32[]{:T(128)S(6)} %select_n.3), kind=kLoop, calls=%fused_computation | loop fusion | bytes 1048580 | tf_op jit(solution)/shard_map/dynamic_slice | solution.py:187
  15.3 0.7 collective-permute-done.3.lh_ref
  16.0 0.0 collective-permute-done.4.rl_ref
  16.0 5.6 %collective-permute-done.2.ll_ref = bf16[32,8,512]{2,1,0:T(8,128)(2,1)S(1)} collective-permute-done((bf16[32,8,512]{2,1,0:T(8,128)(2,1)S(1)}, bf16[32,8,512]{2,1,0:T(8,128)(2,1)S(1)}, u32[]{:S(2)}, u32[]{:S(2)}) %collective-permute-start.2) | collective-permute-done | bytes 262176 | tf_op jit(solution)/shard_map/ppermute | solution.py:185
  21.6 0.3 shard_map.89
  21.9 42.3 %all_to_all.10.arrived_ref = bf16[64,2,8,512]{3,2,1,0:T(8,128)(2,1)S(1)} all-to-all(bf16[64,2,8,512]{3,2,1,0:T(8,128)(2,1)S(1)} %bitcast.13), channel_id=1, replica_groups=mesh['dp'=4,'shard'=64] {'shard'}, dimensions={0} | all-to-all | bytes 2097152 | tf_op jit(solution)/shard_map/all_to_all | solution.py:204
  64.2 2.7 %shard_map.91 = bf16[64,2,8,512]{3,2,1,0:T(8,128)(2,1)} custom-call(bf16[64,2,8,512]{3,2,1,0:T(8,128)(2,1)S(1)} %all_to_all.10.arrived_ref, bf16[2,512,512]{2,1,0:T(8,128)(2,1)S(1)} %bitcast.14, bf16[2,512,512]{2,1,0:T(8,128)(2,1)S(1)} %bitcast.15), custom_call_target="tpu_custom_call" | custom-call | tf_op jit(solution)/shard_map/pallas_call | solution.py:207
  66.9 6.2 %all-to-all-start.1 = ((bf16[64,2,8,512]{3,2,1,0:T(8,128)(2,1)}), bf16[64,2,8,512]{3,2,1,0:T(8,128)(2,1)S(1)}, u32[]{:S(2)}, u32[]{:S(2)}) async-start(bf16[64,2,8,512]{3,2,1,0:T(8,128)(2,1)} %shard_map.91), calls=%async_computation.1 | async-start | bytes 2097152 | tf_op jit(solution)/shard_map/all_to_all | solution.py:219
  73.1 4.4 %shard_map.90 = (f32[2,512,512]{2,1,0:T(8,128)}, f32[2,512,512]{2,1,0:T(8,128)}) custom-call(s32[1]{0:T(128)S(4)} %get-tuple-element.24.count_ref, bf16[64,2,8,512]{3,2,1,0:T(8,128)(2,1)S(1)} %all_to_all.10.arrived_ref, f32[2,512,512]{2,1,0:T(8,128)} %bitcast.19, f32[2,512,512]{2,1,0:T(8,128)} %bitcast.20), custom_call_target="tpu_custom_call" | custom-call | flops 2147483648 | bytes 9437184 | tf_op jit(solution)/shard_map/pallas_call | solution.py:222
  77.5 24.2 %all-to-all-done.1 = bf16[64,2,8,512]{3,2,1,0:T(8,128)(2,1)S(1)} async-done(((bf16[64,2,8,512]{3,2,1,0:T(8,128)(2,1)}), bf16[64,2,8,512]{3,2,1,0:T(8,128)(2,1)S(1)}, u32[]{:S(2)}, u32[]{:S(2)}) %all-to-all-start.1) | async-done | bytes 1048608 | tf_op jit(solution)/shard_map/all_to_all | solution.py:219
  101.6 0.8 shard_map.92
  (6 shorter events, 0.0 us)
Async XLA Ops:
  1.7 11.5 %copy-start.2 = (s32[256,1]{0,1:T(1,128)S(1)}, s32[256,1]{0,1:T(1,128)}, u32[]{:S(2)}) copy-start(s32[256,1]{0,1:T(1,128)} %param.7) | copy-start | bytes 3076
  1.7 7.5 %collective-permute-start = (bf16[32,8,512]{2,1,0:T(8,128)(2,1)S(1)}, bf16[32,8,512]{2,1,0:T(8,128)(2,1)S(1)}, u32[]{:S(2)}, u32[]{:S(2)}) collective-permute-start(bf16[32,8,512]{2,1,0:T(8,128)(2,1)S(1)} %get-tuple-element.20), channel_id=1, source_target_pairs={{0,64},{64,128},{128,192},{192,0},{1,65},{65,129},{129,193},{193,1... | collective-permute-start | bytes 786440 | tf_op jit(solution)/shard_map/ppermute | solution.py:173
  3.8 6.5 %collective-permute-start.1 = (bf16[32,8,512]{2,1,0:T(8,128)(2,1)S(1)}, bf16[32,8,512]{2,1,0:T(8,128)(2,1)S(1)}, u32[]{:S(2)}, u32[]{:S(2)}) collective-permute-start(bf16[32,8,512]{2,1,0:T(8,128)(2,1)S(1)} %get-tuple-element.21), channel_id=1, source_target_pairs={{0,192},{64,0},{128,64},{192,128},{1,193},{65,1},{129,65},{193,129... | collective-permute-start | bytes 786440 | tf_op jit(solution)/shard_map/ppermute | solution.py:174
  6.4 9.6 %collective-permute-start.3 = (bf16[32,8,512]{2,1,0:T(8,128)(2,1)S(1)}, bf16[32,8,512]{2,1,0:T(8,128)(2,1)S(1)}, u32[]{:S(2)}, u32[]{:S(2)}) collective-permute-start(bf16[32,8,512]{2,1,0:T(8,128)(2,1)S(1)} %get-tuple-element.28), channel_id=1, source_target_pairs={{0,64},{64,128},{128,192},{192,0},{1,65},{65,129},{129,193},{193,1... | collective-permute-start | bytes 786440 | tf_op jit(solution)/shard_map/ppermute | solution.py:175
  6.6 9.4 %collective-permute-start.4 = (bf16[32,8,512]{2,1,0:T(8,128)(2,1)S(1)}, bf16[32,8,512]{2,1,0:T(8,128)(2,1)S(1)}, u32[]{:S(2)}, u32[]{:S(2)}) collective-permute-start(bf16[32,8,512]{2,1,0:T(8,128)(2,1)S(1)} %get-tuple-element.29), channel_id=1, source_target_pairs={{0,192},{64,0},{128,64},{192,128},{1,193},{65,1},{129,65},{193,129... | collective-permute-start | bytes 786440 | tf_op jit(solution)/shard_map/ppermute | solution.py:176
  10.5 11.2 %collective-permute-start.2 = (bf16[32,8,512]{2,1,0:T(8,128)(2,1)S(1)}, bf16[32,8,512]{2,1,0:T(8,128)(2,1)S(1)}, u32[]{:S(2)}, u32[]{:S(2)}) collective-permute-start(bf16[32,8,512]{2,1,0:T(8,128)(2,1)S(1)} %get-tuple-element.27), channel_id=1, source_target_pairs={{0,64},{64,128},{128,192},{192,0},{1,65},{65,129},{129,193},{193,1... | collective-permute-start | bytes 786440 | tf_op jit(solution)/shard_map/ppermute | solution.py:185
  12.1 9.5 %collective-permute-start.5 = (bf16[32,8,512]{2,1,0:T(8,128)(2,1)S(1)}, bf16[32,8,512]{2,1,0:T(8,128)(2,1)S(1)}, u32[]{:S(2)}, u32[]{:S(2)}) collective-permute-start(bf16[32,8,512]{2,1,0:T(8,128)(2,1)S(1)} %get-tuple-element.30), channel_id=1, source_target_pairs={{0,192},{64,0},{128,64},{192,128},{1,193},{65,1},{129,65},{193,129... | collective-permute-start | bytes 786440 | tf_op jit(solution)/shard_map/ppermute | solution.py:186
  21.6 42.6 %copy-start = (bf16[1,1,2,512,512]{4,3,2,1,0:T(8,128)(2,1)S(1)}, bf16[1,1,2,512,512]{4,3,2,1,0:T(8,128)(2,1)}, u32[]{:S(2)}) copy-start(bf16[1,1,2,512,512]{4,3,2,1,0:T(8,128)(2,1)} %param.10) | copy-start | bytes 3145732
  21.6 42.6 %copy-start.1 = (bf16[1,1,2,512,512]{4,3,2,1,0:T(8,128)(2,1)S(1)}, bf16[1,1,2,512,512]{4,3,2,1,0:T(8,128)(2,1)}, u32[]{:S(2)}) copy-start(bf16[1,1,2,512,512]{4,3,2,1,0:T(8,128)(2,1)} %param.11) | copy-start | bytes 3145732
  66.9 34.8 %all-to-all-start.1 = ((bf16[64,2,8,512]{3,2,1,0:T(8,128)(2,1)}), bf16[64,2,8,512]{3,2,1,0:T(8,128)(2,1)S(1)}, u32[]{:S(2)}, u32[]{:S(2)}) async-start(bf16[64,2,8,512]{3,2,1,0:T(8,128)(2,1)} %shard_map.91), calls=%async_computation.1 | async-start | bytes 2097152 | tf_op jit(solution)/shard_map/all_to_all | solution.py:219

commit v6 on v5

--- a/solution.py
+++ b/solution.py
@@ -212,7 +212,7 @@
         scratch_shapes=[
             pltpu.VMEM((slots_each, owners * rows, width), jnp.bfloat16),
             pltpu.VMEM((slots_each, owners, rows, width), jnp.bfloat16),
-            pltpu.SemaphoreType.DMA((slots_each, 2)),
+            pltpu.SemaphoreType.DMA((slots_each, 1)),
         ],
         compiler_params=params(),
     )(arrived, left_root[0, 0], right_root[0, 0])

time: 103 us -> 103 us (level)
  no operation moved by 1% of the time
where the time goes in v6:
time: 103 us; the launch traced here: 102 us
  blocking collectives  42.3 us (41%)
  waiting for transfers between devices  31.7 us (31%)
  starting transfers between devices  15.2 us (15%)
  Pallas kernels  11.6 us (11%)
  local copies, waits for them, and re-layouts  1.1 us (1%)
    all_to_all x1, blocking collectives, shards(): lax.all_to_all(outgoing.reshape(owners, slots_each, rows, width), 'shard'...  42.3 us
    all_to_all x1, waiting for transfers between devices, shards(): lax.all_to_all(finished, 'shard', split_axis=0, concat_axis=0, tiled=True)  24.2 us
    all_to_all x1, starting transfers between devices, shards(): lax.all_to_all(finished, 'shard', split_axis=0, concat_axis=0, tiled=True)  6.2 us
    ppermute x1, waiting for transfers between devices, shards(): from_left_low = lax.ppermute(to_right, 'dp', rightward)  5.61 us
    pallas_call x1, Pallas kernels, shards(): pl.pallas_call(factors, grid=(slots_each,), out_shape=[jax.ShapeDtypeStru...  4.37 us
    pallas_call x1, Pallas kernels, shards(): pl.pallas_call(precondition, out_shape=pltpu.HBM((owners, slots_each, row...  2.66 us
    ppermute x1, starting transfers between devices, shards(): from_right_low = lax.ppermute(near_left, 'dp', leftward)  2.57 us
    pallas_call x2, Pallas kernels, staged(): pl.pallas_call(functools.partial(stage, replicas, wanted), out_shape=[pie...  2.28 us
  transfers between devices with their start and end apart: 7, of which 4 were waited for; matrix products, arithmetic and copies ran while one was open for 1% of the time, Pallas kernels for 7%

profile of v6, /device:TPU:1, one launch (start us, length us, event | category | flops | bytes accessed | tf_op | source)
XLA Modules:
  0.0 102.5 jit_solution(10487887196121087010)
XLA Ops:
  0.6 1.1 %shard_map.86 = (bf16[32,8,512]{2,1,0:T(8,128)(2,1)S(1)}, bf16[32,8,512]{2,1,0:T(8,128)(2,1)S(1)}) custom-call(bf16[256,8,512]{2,1,0:T(8,128)(2,1)} %bitcast.17), custom_call_target="tpu_custom_call" | custom-call | tf_op jit(solution)/shard_map/pallas_call | solution.py:162
  1.7 0.0 copy-start.2
  1.7 2.1 %collective-permute-start = (bf16[32,8,512]{2,1,0:T(8,128)(2,1)S(1)}, bf16[32,8,512]{2,1,0:T(8,128)(2,1)S(1)}, u32[]{:S(2)}, u32[]{:S(2)}) collective-permute-start(bf16[32,8,512]{2,1,0:T(8,128)(2,1)S(1)} %get-tuple-element.20), channel_id=1, source_target_pairs={{0,64},{64,128},{128,192},{192,0},{1,65},{65,129},{129,193},{193,1... | collective-permute-start | bytes 786440 | tf_op jit(solution)/shard_map/ppermute | solution.py:173
  3.8 1.4 %collective-permute-start.1 = (bf16[32,8,512]{2,1,0:T(8,128)(2,1)S(1)}, bf16[32,8,512]{2,1,0:T(8,128)(2,1)S(1)}, u32[]{:S(2)}, u32[]{:S(2)}) collective-permute-start(bf16[32,8,512]{2,1,0:T(8,128)(2,1)S(1)} %get-tuple-element.21), channel_id=1, source_target_pairs={{0,192},{64,0},{128,64},{192,128},{1,193},{65,1},{129,65},{193,129... | collective-permute-start | bytes 786440 | tf_op jit(solution)/shard_map/ppermute | solution.py:174
  5.2 1.2 %shard_map.85 = (bf16[32,8,512]{2,1,0:T(8,128)(2,1)S(1)}, bf16[32,8,512]{2,1,0:T(8,128)(2,1)S(1)}, bf16[32,8,512]{2,1,0:T(8,128)(2,1)S(1)}, bf16[32,8,512]{2,1,0:T(8,128)(2,1)S(1)}) custom-call(bf16[256,8,512]{2,1,0:T(8,128)(2,1)} %bitcast.18), custom_call_target="tpu_custom_call" | custom-call | tf_op jit(solution)/shard_map/pallas_call | solution.py:162
  6.4 0.2 collective-permute-start.3
  6.6 2.6 %collective-permute-start.4 = (bf16[32,8,512]{2,1,0:T(8,128)(2,1)S(1)}, bf16[32,8,512]{2,1,0:T(8,128)(2,1)S(1)}, u32[]{:S(2)}, u32[]{:S(2)}) collective-permute-start(bf16[32,8,512]{2,1,0:T(8,128)(2,1)S(1)} %get-tuple-element.29), channel_id=1, source_target_pairs={{0,192},{64,0},{128,64},{192,128},{1,193},{65,1},{129,65},{193,129... | collective-permute-start | bytes 786440 | tf_op jit(solution)/shard_map/ppermute | solution.py:176
  9.2 0.0 collective-permute-done.low_ref
  9.2 1.2 %collective-permute-done.1.high_ref = bf16[32,8,512]{2,1,0:T(8,128)(2,1)S(1)} collective-permute-done((bf16[32,8,512]{2,1,0:T(8,128)(2,1)S(1)}, bf16[32,8,512]{2,1,0:T(8,128)(2,1)S(1)}, u32[]{:S(2)}, u32[]{:S(2)}) %collective-permute-start.1) | collective-permute-done | bytes 262176 | tf_op jit(solution)/shard_map/ppermute | solution.py:174
  10.3 0.1 shard_map.87
  10.5 1.6 %collective-permute-start.2 = (bf16[32,8,512]{2,1,0:T(8,128)(2,1)S(1)}, bf16[32,8,512]{2,1,0:T(8,128)(2,1)S(1)}, u32[]{:S(2)}, u32[]{:S(2)}) collective-permute-start(bf16[32,8,512]{2,1,0:T(8,128)(2,1)S(1)} %get-tuple-element.27), channel_id=1, source_target_pairs={{0,64},{64,128},{128,192},{192,0},{1,65},{65,129},{129,193},{193,1... | collective-permute-start | bytes 786440 | tf_op jit(solution)/shard_map/ppermute | solution.py:185
  12.1 1.1 %collective-permute-start.5 = (bf16[32,8,512]{2,1,0:T(8,128)(2,1)S(1)}, bf16[32,8,512]{2,1,0:T(8,128)(2,1)S(1)}, u32[]{:S(2)}, u32[]{:S(2)}) collective-permute-start(bf16[32,8,512]{2,1,0:T(8,128)(2,1)S(1)} %get-tuple-element.30), channel_id=1, source_target_pairs={{0,192},{64,0},{128,64},{192,128},{1,193},{65,1},{129,65},{193,129... | collective-permute-start | bytes 786440 | tf_op jit(solution)/shard_map/ppermute | solution.py:186
  13.2 1.0 shard_map.88
  14.2 1.1 %dynamic-slice_bitcast_fusion.own_ref = bf16[64,8,512]{2,1,0:T(8,128)(2,1)S(1)} fusion(bf16[1,256,8,512]{3,2,1,0:T(8,128)(2,1)} %param.6, s32[]{:T(128)S(6)} %select_n.3), kind=kLoop, calls=%fused_computation | loop fusion | bytes 1048580 | tf_op jit(solution)/shard_map/dynamic_slice | solution.py:187
  15.3 0.7 collective-permute-done.3.lh_ref
  16.0 0.0 collective-permute-done.4.rl_ref
  16.0 5.6 %collective-permute-done.2.ll_ref = bf16[32,8,512]{2,1,0:T(8,128)(2,1)S(1)} collective-permute-done((bf16[32,8,512]{2,1,0:T(8,128)(2,1)S(1)}, bf16[32,8,512]{2,1,0:T(8,128)(2,1)S(1)}, u32[]{:S(2)}, u32[]{:S(2)}) %collective-permute-start.2) | collective-permute-done | bytes 262176 | tf_op jit(solution)/shard_map/ppermute | solution.py:185
  21.6 0.3 shard_map.89
  21.9 42.3 %all_to_all.10.arrived_ref = bf16[64,2,8,512]{3,2,1,0:T(8,128)(2,1)S(1)} all-to-all(bf16[64,2,8,512]{3,2,1,0:T(8,128)(2,1)S(1)} %bitcast.13), channel_id=1, replica_groups=mesh['dp'=4,'shard'=64] {'shard'}, dimensions={0} | all-to-all | bytes 2097152 | tf_op jit(solution)/shard_map/all_to_all | solution.py:204
  64.2 2.7 %shard_map.91 = bf16[64,2,8,512]{3,2,1,0:T(8,128)(2,1)} custom-call(bf16[64,2,8,512]{3,2,1,0:T(8,128)(2,1)S(1)} %all_to_all.10.arrived_ref, bf16[2,512,512]{2,1,0:T(8,128)(2,1)S(1)} %bitcast.14, bf16[2,512,512]{2,1,0:T(8,128)(2,1)S(1)} %bitcast.15), custom_call_target="tpu_custom_call" | custom-call | tf_op jit(solution)/shard_map/pallas_call | solution.py:207
  66.9 6.2 %all-to-all-start.1 = ((bf16[64,2,8,512]{3,2,1,0:T(8,128)(2,1)}), bf16[64,2,8,512]{3,2,1,0:T(8,128)(2,1)S(1)}, u32[]{:S(2)}, u32[]{:S(2)}) async-start(bf16[64,2,8,512]{3,2,1,0:T(8,128)(2,1)} %shard_map.91), calls=%async_computation.1 | async-start | bytes 2097152 | tf_op jit(solution)/shard_map/all_to_all | solution.py:219
  73.1 4.4 %shard_map.90 = (f32[2,512,512]{2,1,0:T(8,128)}, f32[2,512,512]{2,1,0:T(8,128)}) custom-call(s32[1]{0:T(128)S(4)} %get-tuple-element.24.count_ref, bf16[64,2,8,512]{3,2,1,0:T(8,128)(2,1)S(1)} %all_to_all.10.arrived_ref, f32[2,512,512]{2,1,0:T(8,128)} %bitcast.19, f32[2,512,512]{2,1,0:T(8,128)} %bitcast.20), custom_call_target="tpu_custom_call" | custom-call | flops 2147483648 | bytes 9437184 | tf_op jit(solution)/shard_map/pallas_call | solution.py:222
  77.5 24.2 %all-to-all-done.1 = bf16[64,2,8,512]{3,2,1,0:T(8,128)(2,1)S(1)} async-done(((bf16[64,2,8,512]{3,2,1,0:T(8,128)(2,1)}), bf16[64,2,8,512]{3,2,1,0:T(8,128)(2,1)S(1)}, u32[]{:S(2)}, u32[]{:S(2)}) %all-to-all-start.1) | async-done | bytes 1048608 | tf_op jit(solution)/shard_map/all_to_all | solution.py:219
  101.6 0.8 shard_map.92
  (6 shorter events, 0.0 us)
Async XLA Ops:
  1.7 11.5 %copy-start.2 = (s32[256,1]{0,1:T(1,128)S(1)}, s32[256,1]{0,1:T(1,128)}, u32[]{:S(2)}) copy-start(s32[256,1]{0,1:T(1,128)} %param.7) | copy-start | bytes 3076
  1.7 7.5 %collective-permute-start = (bf16[32,8,512]{2,1,0:T(8,128)(2,1)S(1)}, bf16[32,8,512]{2,1,0:T(8,128)(2,1)S(1)}, u32[]{:S(2)}, u32[]{:S(2)}) collective-permute-start(bf16[32,8,512]{2,1,0:T(8,128)(2,1)S(1)} %get-tuple-element.20), channel_id=1, source_target_pairs={{0,64},{64,128},{128,192},{192,0},{1,65},{65,129},{129,193},{193,1... | collective-permute-start | bytes 786440 | tf_op jit(solution)/shard_map/ppermute | solution.py:173
  3.8 6.5 %collective-permute-start.1 = (bf16[32,8,512]{2,1,0:T(8,128)(2,1)S(1)}, bf16[32,8,512]{2,1,0:T(8,128)(2,1)S(1)}, u32[]{:S(2)}, u32[]{:S(2)}) collective-permute-start(bf16[32,8,512]{2,1,0:T(8,128)(2,1)S(1)} %get-tuple-element.21), channel_id=1, source_target_pairs={{0,192},{64,0},{128,64},{192,128},{1,193},{65,1},{129,65},{193,129... | collective-permute-start | bytes 786440 | tf_op jit(solution)/shard_map/ppermute | solution.py:174
  6.4 9.6 %collective-permute-start.3 = (bf16[32,8,512]{2,1,0:T(8,128)(2,1)S(1)}, bf16[32,8,512]{2,1,0:T(8,128)(2,1)S(1)}, u32[]{:S(2)}, u32[]{:S(2)}) collective-permute-start(bf16[32,8,512]{2,1,0:T(8,128)(2,1)S(1)} %get-tuple-element.28), channel_id=1, source_target_pairs={{0,64},{64,128},{128,192},{192,0},{1,65},{65,129},{129,193},{193,1... | collective-permute-start | bytes 786440 | tf_op jit(solution)/shard_map/ppermute | solution.py:175
  6.6 9.4 %collective-permute-start.4 = (bf16[32,8,512]{2,1,0:T(8,128)(2,1)S(1)}, bf16[32,8,512]{2,1,0:T(8,128)(2,1)S(1)}, u32[]{:S(2)}, u32[]{:S(2)}) collective-permute-start(bf16[32,8,512]{2,1,0:T(8,128)(2,1)S(1)} %get-tuple-element.29), channel_id=1, source_target_pairs={{0,192},{64,0},{128,64},{192,128},{1,193},{65,1},{129,65},{193,129... | collective-permute-start | bytes 786440 | tf_op jit(solution)/shard_map/ppermute | solution.py:176
  10.5 11.2 %collective-permute-start.2 = (bf16[32,8,512]{2,1,0:T(8,128)(2,1)S(1)}, bf16[32,8,512]{2,1,0:T(8,128)(2,1)S(1)}, u32[]{:S(2)}, u32[]{:S(2)}) collective-permute-start(bf16[32,8,512]{2,1,0:T(8,128)(2,1)S(1)} %get-tuple-element.27), channel_id=1, source_target_pairs={{0,64},{64,128},{128,192},{192,0},{1,65},{65,129},{129,193},{193,1... | collective-permute-start | bytes 786440 | tf_op jit(solution)/shard_map/ppermute | solution.py:185
  12.1 9.5 %collective-permute-start.5 = (bf16[32,8,512]{2,1,0:T(8,128)(2,1)S(1)}, bf16[32,8,512]{2,1,0:T(8,128)(2,1)S(1)}, u32[]{:S(2)}, u32[]{:S(2)}) collective-permute-start(bf16[32,8,512]{2,1,0:T(8,128)(2,1)S(1)} %get-tuple-element.30), channel_id=1, source_target_pairs={{0,192},{64,0},{128,64},{192,128},{1,193},{65,1},{129,65},{193,129... | collective-permute-start | bytes 786440 | tf_op jit(solution)/shard_map/ppermute | solution.py:186
  21.6 42.6 %copy-start = (bf16[1,1,2,512,512]{4,3,2,1,0:T(8,128)(2,1)S(1)}, bf16[1,1,2,512,512]{4,3,2,1,0:T(8,128)(2,1)}, u32[]{:S(2)}) copy-start(bf16[1,1,2,512,512]{4,3,2,1,0:T(8,128)(2,1)} %param.10) | copy-start | bytes 3145732
  21.6 42.6 %copy-start.1 = (bf16[1,1,2,512,512]{4,3,2,1,0:T(8,128)(2,1)S(1)}, bf16[1,1,2,512,512]{4,3,2,1,0:T(8,128)(2,1)}, u32[]{:S(2)}) copy-start(bf16[1,1,2,512,512]{4,3,2,1,0:T(8,128)(2,1)} %param.11) | copy-start | bytes 3145732
  66.9 34.8 %all-to-all-start.1 = ((bf16[64,2,8,512]{3,2,1,0:T(8,128)(2,1)}), bf16[64,2,8,512]{3,2,1,0:T(8,128)(2,1)S(1)}, u32[]{:S(2)}, u32[]{:S(2)}) async-start(bf16[64,2,8,512]{3,2,1,0:T(8,128)(2,1)} %shard_map.91), calls=%async_computation.1 | async-start | bytes 2097152 | tf_op jit(solution)/shard_map/all_to_all | solution.py:219
